TPU v7x, 512 devices: a whole 4x8x8 slice. The times are simulated.
512 devices in a mesh: row: 32 (over y_lo, z), col: 16 (over y_hi, x, core).
Axes of the slice: x: 4, y: 8 (y_hi: 2, y_lo: 4; y = y_hi * 4 + y_lo), z: 8, core: 2. Of those that a mesh axis runs over, the one named last changes fastest.
Arguments:
- hamiltonian_blocks: float32 [32, 16, 4, 128, 128], P('row', 'col'), may hold values from -0.25 to 0.25
- block_rows: int32 [32, 16, 4], P('row', 'col'), may hold values from 0 to 31
- block_cols: int32 [32, 16, 4], P('row', 'col'), may hold values from 0 to 31
- current_states: float32 [8, 131072], P(None, 'row'), may hold values from -6 to 6
- previous_steps: float32 [8, 131072], P(None, 'row'), may hold values from -6 to 6
Outputs:
- ritz_basis: float32 [24, 131072], P(None, ('row', 'col'))
- rayleigh_matrix: float32 [24, 24], replicated
All inputs are finite; a program needn't handle non-finite values.
Results may differ from a plain program's by a relative error of at most 0.0003.
Values sent between devices are 32-bit elements; how exact they have to be, the bound alone decides.
A program may use at most 64 MiB of HBM per device.

v0:
```python
import jax
import jax.numpy as jnp
from jax import lax
from jax.sharding import PartitionSpec as P

exactness = lax.Precision.HIGHEST


def passed_along(array, axis, by):
    length = lax.axis_size(axis)
    return lax.ppermute(array, axis, [(i, (i + by) % length) for i in range(length)])


def local_terms(tiles, row_index, col_index, owned, remote):
    positions = jnp.arange(owned.shape[1], dtype=jnp.int32)
    owned_rows = jnp.take(owned, row_index, axis=1)
    remote_cols = jnp.take(remote, col_index, axis=1)
    direct = jnp.einsum("knb,ncb->knc", remote_cols, tiles, precision=exactness)
    mirrored = jnp.einsum("knc,ncb->knb", owned_rows, tiles, precision=exactness)
    row_onehot = (row_index[:, None] == positions[None, :]).astype(jnp.float32)
    col_onehot = (col_index[:, None] == positions[None, :]).astype(jnp.float32)
    into_owned = jnp.einsum("knc,ns->ksc", direct, row_onehot, precision=exactness)
    into_remote = jnp.einsum("knb,ns->ksb", mirrored, col_onehot, precision=exactness)
    return (into_owned, into_remote)


def matmul(left, right):
    return jnp.dot(left, right, precision=exactness)


def body(hamiltonian_blocks, block_rows, block_cols, current_states, previous_steps):
    tiles = hamiltonian_blocks[0, 0]
    row_index = block_rows[0, 0]
    col_index = block_cols[0, 0]
    states = current_states.shape[0]
    seglength = current_states.shape[1]
    blockwidth = tiles.shape[2]
    segblocks = seglength // blockwidth
    grid_rows = lax.axis_size("row")
    grid_cols = lax.axis_size("col")
    my_col = lax.axis_index("col")
    share = seglength // grid_cols
    count = grid_rows * seglength
    bit_count = (grid_cols - 1).bit_length()

    def rows_share(vectors):
        return lax.dynamic_slice_in_dim(vectors, my_col * share, share, 1)

    def fetch(vectors):
        remote = vectors
        for bit_pos in range(bit_count):
            moved = passed_along(remote, "row", -(1 << bit_pos))
            remote = jnp.where((my_col >> bit_pos) % 2 == 1, moved, remote)
        return remote

    def return_terms(terms):
        for bit_pos in range(bit_count):
            moved = passed_along(terms, "row", 1 << bit_pos)
            terms = jnp.where((my_col >> bit_pos) % 2 == 1, moved, terms)
        return terms

    def product(vectors):
        width = vectors.shape[0]
        remote = fetch(vectors)
        into_owned, into_remote = local_terms(
            tiles,
            row_index,
            col_index,
            vectors.reshape(width, segblocks, blockwidth),
            remote.reshape(width, segblocks, blockwidth),
        )
        partial_value = (into_owned + return_terms(into_remote)).reshape(width, seglength)
        full_sum = lax.psum(partial_value, "col")
        return (full_sum, rows_share(full_sum))

    images_full, images_piece = product(current_states)
    states_piece = rows_share(current_states)
    steps_piece = rows_share(previous_steps)
    theta_matrix = lax.psum(matmul(states_piece, images_piece.T), ("row", "col")) / count
    residual_piece = images_piece - matmul(theta_matrix.T, states_piece)
    raw_piece = jnp.concatenate([residual_piece, states_piece, steps_piece], 0)
    gram = lax.psum(matmul(raw_piece, raw_piece.T), ("row", "col")) / count
    lower = jnp.linalg.cholesky(gram)
    identity = jnp.eye(3 * states, dtype=gram.dtype)
    inverse = lax.linalg.triangular_solve(lower, identity, left_side=True, lower=True)
    basis_piece = matmul(inverse, raw_piece)
    residual_full = images_full - matmul(theta_matrix.T, current_states)
    further_full, further_piece = product(jnp.concatenate([residual_full, previous_steps], 0))
    images_all = jnp.concatenate([further_piece[:states], images_piece, further_piece[states:]], 0)
    projected = matmul(inverse, images_all)
    rayleigh = lax.psum(matmul(basis_piece, projected.T), ("row", "col")) / count
    return (basis_piece, rayleigh)


def solution(mesh):
    return jax.shard_map(
        body,
        mesh=mesh,
        in_specs=(
            P("row", "col", None, None, None),
            P("row", "col", None),
            P("row", "col", None),
            P(None, "row"),
            P(None, "row"),
        ),
        out_specs=(P(None, ("row", "col")), P()),
        check_vma=False,
    )
```

profile of v0, /device:TPU:1, one launch (start us, length us, event | category | flops | bytes accessed | tf_op | source)
XLA Modules:
  0.0 820.8 jit_solution(4319350312502889518)
XLA Ops:
  7.2 14.7 %collective-permute-start = (f32[8,4096]{1,0:T(8,128)}, f32[8,4096]{1,0:T(8,128)S(1)}, u32[]{:S(2)}, u32[]{:S(2)}) collective-permute-start(f32[8,4096]{1,0:T(8,128)} %param.12), channel_id=1, source_target_pairs={{0,496},{16,0},{32,16},{48,32},{64,48},{80,64},{96,80},{112,96},{1... | collective-permute-start | bytes 393224 | tf_op jit(solution)/shard_map/ppermute | solution.py:11
  27.5 3.4 collective-permute-start.1
  30.9 4.2 collective-permute-done.4
  35.1 1.9 collective-permute-start.5
  37.0 1.9 collective-permute-start.2
  39.0 8.5 %collective-permute-done.5 = f32[8,32,128]{2,1,0:T(8,128)S(1)} collective-permute-done((f32[8,32,128]{2,1,0:T(8,128)S(1)}, f32[8,32,128]{2,1,0:T(8,128)S(1)}, u32[]{:S(2)}, u32[]{:S(2)}) %collective-permute-start.5) | collective-permute-done | bytes 131104 | tf_op jit(solution)/shard_map/ppermute | solution.py:11
  52.5 7.7 collective-permute-done.6
  63.6 4.1 collective-permute-done.7
  69.4 181.5 %all-reduce.3.cloned.1.call-done = f32[8,4096]{1,0:T(8,128)} async-done(((f32[8,4096]{1,0:T(8,128)}), f32[8,4096]{1,0:T(8,128)}) %all-reduce.3.cloned.1.call-update) | async-done | bytes 131088 | tf_op jit(solution)/shard_map/psum | solution.py:73
  251.9 100.0 %psum.36 = f32[8,8]{1,0:T(8,128)S(1)} all-reduce(f32[8,8]{1,0:T(8,128)S(1)} %fusion.68), channel_id=1, replica_groups=mesh['row'=32,'col'=16] {'row','col'}, use_global_device_ids=true, to_apply=%region_1.3 | all-reduce | flops 64 | bytes 512 | tf_op jit(solution)/shard_map/psum | solution.py:79
  352.2 93.6 %psum.37 = f32[24,24]{0,1:T(8,128)S(1)} all-reduce(f32[24,24]{0,1:T(8,128)S(1)} %fusion.23), channel_id=1, replica_groups=mesh['row'=32,'col'=16] {'row','col'}, use_global_device_ids=true, to_apply=%region_2.4 | all-reduce | flops 576 | bytes 4608 | tf_op jit(solution)/shard_map/psum | solution.py:82
  446.3 5.3 collective-permute-start.8
  451.6 2.2 cholesky.17
  453.8 3.1 collective-permute-done.8
  456.9 4.2 collective-permute-start.9
  462.6 6.9 collective-permute-start.12
  469.5 5.3 collective-permute-done.9
  479.3 16.6 %collective-permute-done.10 = f32[16,4096]{1,0:T(8,128)S(1)} collective-permute-done((f32[16,4096]{1,0:T(8,128)S(1)}, f32[16,4096]{1,0:T(8,128)S(1)}, u32[]{:S(2)}, u32[]{:S(2)}) %collective-permute-start.10) | collective-permute-done | bytes 262176 | tf_op jit(solution)/shard_map/ppermute | solution.py:11
  497.9 8.1 collective-permute-start.14
  509.4 4.4 collective-permute-done.14
  513.8 6.3 collective-permute-start.15
  521.0 2.3 collective-permute-done.15
  524.7 187.4 %all-reduce.5.cloned.1.call-done = f32[16,4096]{1,0:T(8,128)} async-done(((f32[16,4096]{1,0:T(8,128)}), f32[16,4096]{1,0:T(8,128)}) %all-reduce.5.cloned.1.call-update) | async-done | bytes 262160 | tf_op jit(solution)/shard_map/psum | solution.py:73
  713.1 100.2 %psum.39 = f32[24,24]{0,1:T(8,128)S(1)} all-reduce(f32[24,24]{0,1:T(8,128)S(1)} %fusion.69), channel_id=1, replica_groups=mesh['row'=32,'col'=16] {'row','col'}, use_global_device_ids=true, to_apply=%region_6.9 | all-reduce | flops 576 | bytes 4608 | tf_op jit(solution)/shard_map/psum | solution.py:91
  (91 shorter events, 32.6 us)
Async XLA Ops:
  7.2 16.9 %copy-start = (f32[1,1,4,128,128]{4,3,2,1,0:T(8,128)S(1)}, f32[1,1,4,128,128]{4,3,2,1,0:T(8,128)}, u32[]{:S(2)}) copy-start(f32[1,1,4,128,128]{4,3,2,1,0:T(8,128)} %param.9) | copy-start | bytes 786436
  7.2 15.4 %copy-start.6 = (s32[1,1,4]{2,1,0:T(1,128)S(1)}, s32[1,1,4]{2,1,0:T(1,128)}, u32[]{:S(2)}) copy-start(s32[1,1,4]{2,1,0:T(1,128)} %param.10) | copy-start | bytes 52
  7.2 243.8 %all-reduce.3.cloned.1.call-start = ((), (), s32[]{:S(2)}) async-start(), calls=%async_computation | async-start | bytes 262144 | tf_op jit(solution)/shard_map/psum | solution.py:73
  7.2 20.2 %collective-permute-start = (f32[8,4096]{1,0:T(8,128)}, f32[8,4096]{1,0:T(8,128)S(1)}, u32[]{:S(2)}, u32[]{:S(2)}) collective-permute-start(f32[8,4096]{1,0:T(8,128)} %param.12), channel_id=1, source_target_pairs={{0,496},{16,0},{32,16},{48,32},{64,48},{80,64},{96,80},{112,96},{1... | collective-permute-start | bytes 393224 | tf_op jit(solution)/shard_map/ppermute | solution.py:11
  25.1 2.4 copy-start.1
  25.4 9.6 %collective-permute-start.4 = (f32[8,32,128]{2,1,0:T(8,128)S(1)}, f32[8,32,128]{2,1,0:T(8,128)S(1)}, u32[]{:S(2)}, u32[]{:S(2)}) collective-permute-start(f32[8,32,128]{2,1,0:T(8,128)S(1)} %convolution_bitcast_fusion.2), channel_id=1, source_target_pairs={{0,16},{16,32},{32,48},{48,64},{64,80},{80,96},{96,112},{112,128},... | collective-permute-start | bytes 393224 | tf_op jit(solution)/shard_map/ppermute | solution.py:11
  27.5 9.5 %collective-permute-start.1 = (f32[8,4096]{1,0:T(8,128)S(1)}, f32[8,4096]{1,0:T(8,128)S(1)}, u32[]{:S(2)}, u32[]{:S(2)}) collective-permute-start(f32[8,4096]{1,0:T(8,128)S(1)} %broadcast_select_fusion.9), channel_id=1, source_target_pairs={{0,480},{16,496},{32,0},{48,16},{64,32},{80,48},{96,64},{112,80},{... | collective-permute-start | bytes 393224 | tf_op jit(solution)/shard_map/ppermute | solution.py:11
  35.1 12.4 %collective-permute-start.5 = (f32[8,32,128]{2,1,0:T(8,128)S(1)}, f32[8,32,128]{2,1,0:T(8,128)S(1)}, u32[]{:S(2)}, u32[]{:S(2)}) collective-permute-start(f32[8,32,128]{2,1,0:T(8,128)S(1)} %broadcast_select_fusion.6), channel_id=1, source_target_pairs={{0,32},{16,48},{32,64},{48,80},{64,96},{80,112},{96,128},{112,144}... | collective-permute-start | bytes 393224 | tf_op jit(solution)/shard_map/ppermute | solution.py:11
  37.0 13.5 %collective-permute-start.2 = (f32[8,4096]{1,0:T(8,128)S(1)}, f32[8,4096]{1,0:T(8,128)S(1)}, u32[]{:S(2)}, u32[]{:S(2)}) collective-permute-start(f32[8,4096]{1,0:T(8,128)S(1)} %broadcast_select_fusion.10), channel_id=1, source_target_pairs={{0,448},{16,464},{32,480},{48,496},{64,0},{80,16},{96,32},{112,48}... | collective-permute-start | bytes 393224 | tf_op jit(solution)/shard_map/ppermute | solution.py:11
  47.5 12.7 %collective-permute-start.6 = (f32[8,32,128]{2,1,0:T(8,128)S(1)}, f32[8,32,128]{2,1,0:T(8,128)S(1)}, u32[]{:S(2)}, u32[]{:S(2)}) collective-permute-start(f32[8,32,128]{2,1,0:T(8,128)S(1)} %broadcast_select_fusion.7), channel_id=1, source_target_pairs={{0,64},{16,80},{32,96},{48,112},{64,128},{80,144},{96,160},{112,17... | collective-permute-start | bytes 393224 | tf_op jit(solution)/shard_map/ppermute | solution.py:11
  50.6 11.5 %collective-permute-start.3 = (f32[8,4096]{1,0:T(8,128)S(1)}, f32[8,4096]{1,0:T(8,128)S(1)}, u32[]{:S(2)}, u32[]{:S(2)}) collective-permute-start(f32[8,4096]{1,0:T(8,128)S(1)} %broadcast_select_fusion.11), channel_id=1, source_target_pairs={{0,384},{16,400},{32,416},{48,432},{64,448},{80,464},{96,480},{112... | collective-permute-start | bytes 393224 | tf_op jit(solution)/shard_map/ppermute | solution.py:11
  60.2 7.5 collective-permute-start.7
  68.5 0.9 copy-start.2
  68.5 643.5 %all-reduce.5.cloned.1.call-start = ((), (), s32[]{:S(2)}) async-start(), calls=%async_computation.1 | async-start | bytes 524288 | tf_op jit(solution)/shard_map/psum | solution.py:73
  251.0 195.0 %copy-start.3 = (f32[8,4096]{1,0:T(8,128)S(1)}, f32[8,4096]{1,0:T(8,128)}, u32[]{:S(2)}) copy-start(f32[8,4096]{1,0:T(8,128)} %all-reduce.3.cloned.1.call-done) | copy-start | bytes 393220
  446.3 10.6 %collective-permute-start.8 = (f32[16,4096]{1,0:T(8,128)S(1)}, f32[16,4096]{1,0:T(8,128)S(1)}, u32[]{:S(2)}, u32[]{:S(2)}) collective-permute-start(f32[16,4096]{1,0:T(8,128)S(1)} %pad_maximum_fusion), channel_id=1, source_target_pairs={{0,496},{16,0},{32,16},{48,32},{64,48},{80,64},{96,80},{112,96},{1... | collective-permute-start | bytes 786440 | tf_op jit(solution)/shard_map/ppermute | solution.py:11
  456.9 17.8 %collective-permute-start.9 = (f32[16,4096]{1,0:T(8,128)S(1)}, f32[16,4096]{1,0:T(8,128)S(1)}, u32[]{:S(2)}, u32[]{:S(2)}) collective-permute-start(f32[16,4096]{1,0:T(8,128)S(1)} %get-tuple-element.11), channel_id=1, source_target_pairs={{0,480},{16,496},{32,0},{48,16},{64,32},{80,48},{96,64},{112,80},{... | collective-permute-start | bytes 786440 | tf_op jit(solution)/shard_map/ppermute | solution.py:11
  462.6 14.8 %collective-permute-start.12 = (f32[16,32,128]{2,1,0:T(8,128)S(1)}, f32[16,32,128]{2,1,0:T(8,128)S(1)}, u32[]{:S(2)}, u32[]{:S(2)}) collective-permute-start(f32[16,32,128]{2,1,0:T(8,128)S(1)} %convolution_bitcast_fusion), channel_id=1, source_target_pairs={{0,16},{16,32},{32,48},{48,64},{64,80},{80,96},{96,112},{112,128},... | collective-permute-start | bytes 786440 | tf_op jit(solution)/shard_map/ppermute | solution.py:11
  474.8 21.1 %collective-permute-start.10 = (f32[16,4096]{1,0:T(8,128)S(1)}, f32[16,4096]{1,0:T(8,128)S(1)}, u32[]{:S(2)}, u32[]{:S(2)}) collective-permute-start(f32[16,4096]{1,0:T(8,128)S(1)} %broadcast_select_fusion.4), channel_id=1, source_target_pairs={{0,448},{16,464},{32,480},{48,496},{64,0},{80,16},{96,32},{112,48}... | collective-permute-start | bytes 786440 | tf_op jit(solution)/shard_map/ppermute | solution.py:11
  477.4 20.5 %collective-permute-start.13 = (f32[16,32,128]{2,1,0:T(8,128)S(1)}, f32[16,32,128]{2,1,0:T(8,128)S(1)}, u32[]{:S(2)}, u32[]{:S(2)}) collective-permute-start(f32[16,32,128]{2,1,0:T(8,128)S(1)} %broadcast_select_fusion), channel_id=1, source_target_pairs={{0,32},{16,48},{32,64},{48,80},{64,96},{80,112},{96,128},{112,144}... | collective-permute-start | bytes 786440 | tf_op jit(solution)/shard_map/ppermute | solution.py:11
  495.9 12.9 %collective-permute-start.11 = (f32[16,4096]{1,0:T(8,128)S(1)}, f32[16,4096]{1,0:T(8,128)S(1)}, u32[]{:S(2)}, u32[]{:S(2)}) collective-permute-start(f32[16,4096]{1,0:T(8,128)S(1)} %broadcast_select_fusion.5), channel_id=1, source_target_pairs={{0,384},{16,400},{32,416},{48,432},{64,448},{80,464},{96,480},{112... | collective-permute-start | bytes 786440 | tf_op jit(solution)/shard_map/ppermute | solution.py:11
  497.9 15.8 %collective-permute-start.14 = (f32[16,32,128]{2,1,0:T(8,128)S(1)}, f32[16,32,128]{2,1,0:T(8,128)S(1)}, u32[]{:S(2)}, u32[]{:S(2)}) collective-permute-start(f32[16,32,128]{2,1,0:T(8,128)S(1)} %broadcast_select_fusion.1), channel_id=1, source_target_pairs={{0,64},{16,80},{32,96},{48,112},{64,128},{80,144},{96,160},{112,17... | collective-permute-start | bytes 786440 | tf_op jit(solution)/shard_map/ppermute | solution.py:11
  513.8 9.6 %collective-permute-start.15 = (f32[16,32,128]{2,1,0:T(8,128)S(1)}, f32[16,32,128]{2,1,0:T(8,128)S(1)}, u32[]{:S(2)}, u32[]{:S(2)}) collective-permute-start(f32[16,32,128]{2,1,0:T(8,128)S(1)} %broadcast_select_fusion.2), channel_id=1, source_target_pairs={{0,128},{16,144},{32,160},{48,176},{64,192},{80,208},{96,224},{112... | collective-permute-start | bytes 786440 | tf_op jit(solution)/shard_map/ppermute | solution.py:11
  524.7 188.3 %copy-start.4 = (f32[24,256]{1,0:T(8,128)}, f32[24,256]{1,0:T(8,128)S(1)}, u32[]{:S(2)}) copy-start(f32[24,256]{1,0:T(8,128)S(1)} %fusion.22) | copy-start | bytes 73732
  (1 other events, 0.7 us)
Sparse Core Ops, SparseCore 0:
  68.7 182.2 all-reduce.2
  524.4 187.5 all-reduce.4
where the time goes:
time: 822 us; the launch traced here: 821 us
  waiting for transfers between devices  426 us (52%)
  blocking collectives  294 us (36%)
  starting transfers between devices  66.2 us (8%)
  between operations  14.6 us (2%)
  local copies, waits for them, and re-layouts  8.49 us (1%)
    psum x2, waiting for transfers between devices, product(): full_sum = lax.psum(partial_value, 'col')  369 us
    psum x1, blocking collectives, body(): lax.psum(matmul(basis_piece, projected.T), ('row', 'col')) / count  100 us
    psum x1, blocking collectives, body(): lax.psum(matmul(states_piece, images_piece.T), ('row', 'col')) / count  100 us
    psum x1, blocking collectives, body(): gram = lax.psum(matmul(raw_piece, raw_piece.T), ('row', 'col')) / count  93.6 us
    ppermute x16, starting transfers between devices, passed_along(): lax.ppermute(array, axis, [(i, (i + by) % length) for i in range(length)])  66.1 us
    ppermute x16, waiting for transfers between devices, passed_along(): lax.ppermute(array, axis, [(i, (i + by) % length) for i in range(length)])  57.5 us
  transfers between devices with their start and end apart: 18, of which 13 were waited for; matrix products, arithmetic and copies ran while one was open for 2% of the time, Pallas kernels for 0%

commit v1 on v0

v1 whole, which is shorter than its diff:
```python
import functools

import jax
import jax.numpy as jnp
from jax import lax
from jax.experimental import pallas as pl
from jax.experimental.pallas import tpu as pltpu
from jax.sharding import PartitionSpec as P

MESH = pl.DeviceIdType.MESH
F32 = jnp.float32
exactness = lax.Precision.HIGHEST

Z, YL, YH, L = 8, 4, 2, 8
Y = YL * YH
N_ROW, N_COL = Z * YL, L * YH
K, B, SEGB, NB = 8, 128, 32, 4
SEG = SEGB * B
SHARE = SEG // N_COL
ROWS = N_ROW * SEG
rem, div = lax.rem, lax.div


def nn(a, b):
    return jnp.dot(a, b, precision=exactness, preferred_element_type=F32)


def nt(a, b):
    return lax.dot_general(a, b, (((1,), (1,)), ((), ())), precision=exactness, preferred_element_type=F32)


def lane_ids(shape):
    return lax.broadcasted_iota(jnp.int32, shape, 1)


def row_ids(shape):
    return lax.broadcasted_iota(jnp.int32, shape, 0)


def padded(a):
    return jnp.concatenate([a, jnp.zeros((B - a.shape[0], a.shape[1]), F32)], 0)


def transposed(a):
    n = a.shape[0]
    unit = (lane_ids((n, n)) == row_ids((n, n))).astype(F32)
    return nt(unit, a[:, :n])


def packed(a):
    return a[0:8] + pltpu.roll(a[8:16], 32, 1) + pltpu.roll(a[16:24], 64, 1)


def unpacked(t):
    a = jnp.concatenate([t, pltpu.roll(t, 96, 1), pltpu.roll(t, 64, 1)], 0)
    return jnp.where(lane_ids(a.shape) < 24, a, 0.0)


def inverse_factor(gram):
    rows, lanes = row_ids(gram.shape), lane_ids(gram.shape)
    left = gram
    right = (rows == lanes).astype(F32)
    for j in range(24):
        pivot = left[j : j + 1, j : j + 1]
        factor = jnp.where(rows[:, :1] > j, left[:, j : j + 1] / pivot, 0.0)
        top, unit = left[j : j + 1], right[j : j + 1]
        left = left - factor * top
        right = right - factor * unit
    diagonal = jnp.sum(jnp.where(rows == lanes, left, 0.0), 1, keepdims=True)
    return right / jnp.sqrt(diagonal)


def kernel(rows_ref, cols_ref, h_ref, x_ref, p_ref, q_ref, ray_ref,
           h, x, x_far, p, p_far, d, m, got_d, got_m, piece, y, y_far, mine, buf_a, buf_b,
           load_sem, x_sem, p_sem, xs_sem, ps_sem, d_sem, m_sem, ds_sem, ms_sem,
           y_sem, yfar_sem, ys_sem, yfs_sem, a_sem, b_sem, as_sem, bs_sem, step2, step3):
    r, c = lax.axis_index("row"), lax.axis_index("col")
    z, y_lo, l, y_hi = rem(r, Z), div(r, Z), rem(c, L), div(c, L)
    yy = y_hi * YL + y_lo

    def at(y_at, z_at, l_at):
        return (rem(y_at, YL) * Z + z_at, div(y_at, YL) * L + l_at)

    def send(src, dst, ss, rs, dev):
        pltpu.make_async_remote_copy(src_ref=src, dst_ref=dst, send_sem=ss, recv_sem=rs,
                                     device_id=dev, device_id_type=MESH).start()

    def done(ref, sem):
        pltpu.make_async_copy(ref, ref, sem).wait()

    q = rem(r + c, N_ROW)
    source = at(rem(yy + y_hi + div(z + l, Z), Y), rem(z + l, Z), l)
    users = []
    for hi in range(YH):
        u_row = rem(r + 2 * N_ROW - L * hi - l, N_ROW)
        u_y = rem(YL * hi + div(u_row, Z) + hi + div(rem(u_row, Z) + l, Z), Y)
        here = u_y == yy
        if hi == 0:
            here = jnp.logical_and(here, l != 0)
        users.append((here, (u_row, L * hi + l)))
    reads = c != 0

    barrier = pltpu.get_barrier_semaphore()

    @pl.when(reads)
    def _():
        pl.semaphore_signal(barrier, inc=1, device_id=source, device_id_type=MESH)

    def greet(n, sem, place):
        def one(k, carry):
            pl.semaphore_signal(sem, inc=1, device_id=place(k), device_id_type=MESH)
            return carry
        lax.fori_loop(1, n, one, 0)

    greet(Z, barrier, lambda k: at(yy, rem(z + k, Z), l))
    greet(Y, barrier, lambda k: at(rem(yy + k, Y), z, l))
    greet(L, barrier, lambda k: at(yy, z, rem(l + k, L)))

    pltpu.make_async_copy(h_ref, h, load_sem.at[0]).start()
    pltpu.make_async_copy(x_ref, x, load_sem.at[1]).start()
    pltpu.make_async_copy(p_ref, p, load_sem.at[2]).start()

    users_here = users[0][0].astype(jnp.int32) + users[1][0].astype(jnp.int32)
    pl.semaphore_wait(barrier, Z - 1 + Y - 1 + L - 1 + users_here)

    for i, (here, place) in enumerate(users):
        @pl.when(here)
        def _(i=i, place=place):
            send(x_ref, x_far, xs_sem.at[i], x_sem, place)

    @pl.when(jnp.logical_not(reads))
    def _():
        pltpu.make_async_copy(x_ref, x_far, x_sem).start()
        pltpu.make_async_copy(p_ref, p_far, p_sem).start()

    greet(Y, step2, lambda k: at(rem(yy + k, Y), z, l))
    pl.semaphore_wait(step2, Y - 1)
    greet(Z, step3, lambda k: at(yy, rem(z + k, Z), l))
    pltpu.make_async_copy(h_ref, h, load_sem.at[0]).wait()
    pltpu.make_async_copy(x_ref, x, load_sem.at[1]).wait()
    pltpu.make_async_copy(p_ref, p, load_sem.at[2]).wait()

    def blocks(ref, places):
        found = [ref[:, :B]] * NB
        for b in range(1, SEGB):
            here = ref[:, b * B : (b + 1) * B]
            found = [jnp.where(places[n] == b, here, found[n]) for n in range(NB)]
        return found

    def spread(terms, places, out):
        for b in range(SEGB):
            total = jnp.where(places[0] == b, terms[0], 0.0)
            for n in range(1, NB):
                total = total + jnp.where(places[n] == b, terms[n], 0.0)
            out[:, b * B : (b + 1) * B] = total

    row_at = [jnp.full((K, B), rows_ref[n], jnp.int32) for n in range(NB)]
    col_at = [jnp.full((K, B), cols_ref[n], jnp.int32) for n in range(NB)]
    x_row, p_row = blocks(x, row_at), blocks(p, row_at)
    both = [nn(jnp.concatenate([x_row[n], p_row[n]], 0), h[n]) for n in range(NB)]
    spread([both[n][:K] for n in range(NB)], col_at, m)

    pl.semaphore_wait(step3, Z - 1)

    def send_m(k, carry):
        j = rem(c + k, N_COL)
        src, dst = m.at[:, pl.ds(pl.multiple_of(j * SHARE, SHARE), SHARE)], got_m.at[c]
        local = jnp.logical_and(c == 0, k == 0)

        @pl.when(local)
        def _():
            pltpu.make_async_copy(src, dst, m_sem).start()

        @pl.when(jnp.logical_not(local))
        def _():
            send(src, dst, ms_sem, m_sem, (q, j))
        return carry

    lax.fori_loop(0, N_COL, send_m, 0)

    done(x_far, x_sem)
    x_col = blocks(x_far, col_at)
    direct = [nt(x_col[n], h[n]) for n in range(NB)]
    spread(direct, row_at, d)

    def send_d(k, carry):
        j = rem(c + k, N_COL)
        send(d.at[:, pl.ds(pl.multiple_of(j * SHARE, SHARE), SHARE)], got_d.at[c], ds_sem, d_sem, (r, j))
        return carry

    own = pl.ds(pl.multiple_of(c * SHARE, SHARE), SHARE)
    pltpu.make_async_copy(d.at[:, own], got_d.at[c], d_sem).start()
    lax.fori_loop(1, N_COL, send_d, 0)

    y_par, y_pair = rem(yy, 2), div(yy, 2)
    slot_a = y_par * L + l
    slot_b = y_pair * Z + z

    def first(i, tile):
        mine[i, 0] = tile
        pltpu.make_async_copy(mine.at[i, 0], buf_a.at[i, slot_a], a_sem.at[i]).start()

        def one(k, carry):
            y_to = 2 * y_pair + rem(y_par + div(k, L), 2)
            send(mine.at[i, 0], buf_a.at[i, slot_a], as_sem.at[i], a_sem.at[i], at(y_to, z, rem(l + k, L)))
            return carry
        lax.fori_loop(1, 2 * L, one, 0)

    def second(i):
        done(buf_a.at[i], a_sem.at[i])
        total = buf_a[i, 0]
        for s in range(1, 2 * L):
            total = total + buf_a[i, s]
        mine[i, 1] = total
        pltpu.make_async_copy(mine.at[i, 1], buf_b.at[i, slot_b], b_sem.at[i]).start()

        def one(k, carry):
            y_to = 2 * rem(y_pair + div(k, Z), Y // 2) + y_par
            send(mine.at[i, 1], buf_b.at[i, slot_b], bs_sem.at[i], b_sem.at[i], at(y_to, rem(z + k, Z), l))
            return carry
        lax.fori_loop(1, Z * Y // 2, one, 0)

    def third(i):
        done(buf_b.at[i], b_sem.at[i])
        total = buf_b[i, 0]
        for s in range(1, Z * Y // 2):
            total = total + buf_b[i, s]
        return total

    m_x = jnp.concatenate([both[n][:K] for n in range(NB)], 1)
    m_p = jnp.concatenate([both[n][K:] for n in range(NB)], 1)
    xc = jnp.concatenate(x_col, 1)
    first(0, nt(m_x, padded(xc)))

    for i, (here, place) in enumerate(users):
        @pl.when(here)
        def _(i=i, place=place):
            send(p_ref, p_far, ps_sem.at[i], p_sem, place)

    second(0)

    done(got_m, m_sem)
    done(got_d, d_sem)
    total = got_d[0]
    for s in range(1, N_COL):
        total = total + got_d[s]
    for s in range(N_COL):
        total = total + got_m[s]
    piece[...] = total
    pltpu.make_async_copy(piece, y.at[:, own], y_sem).start()

    def send_y(k, carry):
        local = jnp.logical_and(c == 0, k == 0)

        @pl.when(local)
        def _():
            pltpu.make_async_copy(piece, y_far.at[:, own], yfar_sem).start()

        @pl.when(jnp.logical_not(local))
        def _():
            send(piece, y_far.at[:, own], yfs_sem, yfar_sem, (rem(r + N_ROW - k, N_ROW), k))

        @pl.when(k != 0)
        def _():
            send(piece, y.at[:, own], ys_sem, y_sem, (r, rem(c + k, N_COL)))
        return carry

    lax.fori_loop(0, N_COL, send_y, 0)

    cross = third(0)[:, :K]
    theta = (cross + transposed(cross)) / ROWS
    x_own, p_own = x[:, own], p[:, own]
    taken = nn(theta, jnp.concatenate(x_row + x_col + [x_own], 1))
    basis = jnp.concatenate([total - taken[:, 2 * NB * B :], x_own, p_own], 0)
    first(1, packed(nt(basis, padded(basis))))

    done(p_far, p_sem)
    p_col = jnp.concatenate(blocks(p_far, col_at), 1)
    second(1)

    done(y, y_sem)
    y_row = blocks(y, row_at)
    m_r = jnp.concatenate([nn(y_row[n] - taken[:, n * B : (n + 1) * B], h[n]) for n in range(NB)], 1)

    done(y_far, yfar_sem)
    r_col = jnp.concatenate(blocks(y_far, col_at), 1) - taken[:, NB * B : 2 * NB * B]
    first(2, packed(nt(jnp.concatenate([m_r, m_x, m_p], 0), padded(jnp.concatenate([r_col, xc, p_col], 0)))))
    second(2)

    inverse = inverse_factor(unpacked(third(1)) / ROWS)[:, :24]
    q_ref[...] = nn(inverse, basis)

    half = unpacked(third(2))[:, :24]
    ray_ref[...] = nt(nn(inverse, (half + transposed(half)) / ROWS), inverse)

    for i, (here, place) in enumerate(users):
        @pl.when(here)
        def _(i=i):
            done(x_ref, xs_sem.at[i])
            done(p_ref, ps_sem.at[i])

    @pl.when(reads)
    def _():
        done(got_m, ms_sem)
        done(got_m, yfs_sem)

    @pl.when(jnp.logical_not(reads))
    def _():
        done(got_m.at[pl.ds(0, N_COL - 1)], ms_sem)
        done(got_m.at[pl.ds(0, N_COL - 1)], yfs_sem)

    done(got_d.at[pl.ds(0, N_COL - 1)], ds_sem)
    done(got_d.at[pl.ds(0, N_COL - 1)], ys_sem)
    for i in range(3):
        done(buf_a.at[i, pl.ds(0, 2 * L - 1)], as_sem.at[i])
        done(buf_b.at[i, pl.ds(0, Z * Y // 2 - 1)], bs_sem.at[i])


def body(hamiltonian_blocks, block_rows, block_cols, current_states, previous_steps):
    vmem, smem, anywhere = (pl.BlockSpec(memory_space=s) for s in (pltpu.VMEM, pltpu.SMEM, pl.ANY))
    dma, regular = pltpu.SemaphoreType.DMA, pltpu.SemaphoreType.REGULAR
    return pl.pallas_call(
        kernel,
        out_shape=(jax.ShapeDtypeStruct((3 * K, SHARE), F32), jax.ShapeDtypeStruct((3 * K, 3 * K), F32)),
        in_specs=[smem, smem, anywhere, anywhere, anywhere],
        out_specs=(vmem, vmem),
        scratch_shapes=[
            pltpu.VMEM((NB, B, B), F32),
            pltpu.VMEM((K, SEG), F32),
            pltpu.VMEM((K, SEG), F32),
            pltpu.VMEM((K, SEG), F32),
            pltpu.VMEM((K, SEG), F32),
            pltpu.VMEM((K, SEG), F32),
            pltpu.VMEM((K, SEG), F32),
            pltpu.VMEM((N_COL, K, SHARE), F32),
            pltpu.VMEM((N_COL, K, SHARE), F32),
            pltpu.VMEM((K, SHARE), F32),
            pltpu.VMEM((K, SEG), F32),
            pltpu.VMEM((K, SEG), F32),
            pltpu.VMEM((3, 2, 8, B), F32),
            pltpu.VMEM((3, 2 * L, 8, B), F32),
            pltpu.VMEM((3, Z * Y // 2, 8, B), F32),
            dma((3,)), dma, dma, dma((2,)), dma((2,)), dma, dma, dma, dma,
            dma, dma, dma, dma, dma((3,)), dma((3,)), dma((3,)), dma((3,)), regular, regular,
        ],
        compiler_params=pltpu.CompilerParams(collective_id=0, has_side_effects=True, vmem_limit_bytes=32 * 1024 * 1024),
        name="lobpcg_step",
    )(block_rows.reshape(NB), block_cols.reshape(NB), hamiltonian_blocks.reshape(NB, B, B), current_states, previous_steps)


def solution(mesh):
    return jax.shard_map(
        body,
        mesh=mesh,
        in_specs=(
            P("row", "col", None, None, None),
            P("row", "col", None),
            P("row", "col", None),
            P(None, "row"),
            P(None, "row"),
        ),
        out_specs=(P(None, ("row", "col")), P()),
        check_vma=False,
    )
```

time: 822 us -> 75.9 us (0.09)
  waiting for transfers between devices: 426 us -> 0 us
  blocking collectives: 294 us -> 0 us
  Pallas kernels: 0 us -> 70.4 us
  starting transfers between devices: 66.2 us -> 0 us
  between operations: 14.6 us -> 0.66 us
    psum x2 -> x0, waiting for transfers between devices: 369 us -> none  [product(): full_sum = lax.psum(partial_value, 'col')]
    psum x3 -> x0, blocking collectives: 294 us -> none  [the longest x1 100 us: body(): lax.psum(matmul(basis_piece, projected.T), ('row', 'col')) / count]
    pallas_call x0 -> x1, Pallas kernels: none -> 70.4 us  [body(): pl.pallas_call(kernel, out_shape=(jax.ShapeDtypeStruct((3 * K, SHARE), F3...]
    ppermute x16 -> x0, starting transfers between devices: 66.1 us -> none  [passed_along(): lax.ppermute(array, axis, [(i, (i + by) % length) for i in range(length)])]
    ppermute x16 -> x0, waiting for transfers between devices: 57.5 us -> none  [passed_along(): lax.ppermute(array, axis, [(i, (i + by) % length) for i in range(length)])]
  transfers between devices with their start and end apart: 18 -> 0, of which waited for: 13 -> 0; matrix products, arithmetic and copies ran while one was open for 2% -> 0% of each run, Pallas kernels for 0% -> 0%
where the time goes in v1:
time: 75.9 us; the launch traced here: 75.7 us
  Pallas kernels  70.4 us (93%)
  local copies, waits for them, and re-layouts  4.62 us (6%)
    pallas_call x1, Pallas kernels, body(): pl.pallas_call(kernel, out_shape=(jax.ShapeDtypeStruct((3 * K, SHARE), F3...  70.4 us
    unnamed x12, local copies, waits for them, and re-layouts  4.62 us

profile of v1, /device:TPU:1, one launch (start us, length us, event | category | flops | bytes accessed | tf_op | source)
XLA Modules:
  0.0 75.7 jit_solution(15797405259541163169)
XLA Ops:
  0.6 0.0 copy-start.3
  0.6 0.0 copy-start.4
  0.7 0.6 copy-done.3
  1.3 0.0 copy-done.4
  1.3 0.0 copy-start
  1.3 0.9 %copy-done = f32[1,1,4,128,128]{4,3,2,1,0:T(8,128)S(1)} copy-done((f32[1,1,4,128,128]{4,3,2,1,0:T(8,128)S(1)}, f32[1,1,4,128,128]{4,3,2,1,0:T(8,128)}, u32[]{:S(2)}) %copy-start) | copy-done | bytes 262168
  2.3 0.0 copy-start.1
  2.3 0.9 %copy-done.1 = f32[8,4096]{1,0:T(8,128)S(1)} copy-done((f32[8,4096]{1,0:T(8,128)S(1)}, f32[8,4096]{1,0:T(8,128)}, u32[]{:S(2)}) %copy-start.1) | copy-done | bytes 131096
  3.2 0.0 copy-start.2
  3.2 0.9 %copy-done.2 = f32[8,4096]{1,0:T(8,128)S(1)} copy-done((f32[8,4096]{1,0:T(8,128)S(1)}, f32[8,4096]{1,0:T(8,128)}, u32[]{:S(2)}) %copy-start.2) | copy-done | bytes 131096
  4.1 70.4 %lobpcg_step.1 = (f32[24,256]{1,0:T(8,128)S(1)}, f32[24,24]{1,0:T(8,128)S(1)}) custom-call(s32[4]{0:T(128)S(1)} %bitcast.4, s32[4]{0:T(128)S(1)} %bitcast.5, f32[4,128,128]{2,1,0:T(8,128)S(1)} %bitcast.3, f32[8,4096]{1,0:T(8,128)S(1)} %copy-done.1, f32[8,4096]{1,0:T(8,128)S(1)} %copy-done.2), custom_call_target="tpu_custom_call" | custom-call | tf_op jit(solution)/shard_map/lobpcg_step/pallas_call | solution.py:322
  74.5 0.6 copy.9
  75.1 0.6 copy.10
Async XLA Ops:
  0.6 0.7 copy-start.3
  0.6 0.7 copy-start.4
  1.3 0.9 %copy-start = (f32[1,1,4,128,128]{4,3,2,1,0:T(8,128)S(1)}, f32[1,1,4,128,128]{4,3,2,1,0:T(8,128)}, u32[]{:S(2)}) copy-start(f32[1,1,4,128,128]{4,3,2,1,0:T(8,128)} %param.5) | copy-start | bytes 786436
  2.3 0.9 %copy-start.1 = (f32[8,4096]{1,0:T(8,128)S(1)}, f32[8,4096]{1,0:T(8,128)}, u32[]{:S(2)}) copy-start(f32[8,4096]{1,0:T(8,128)} %x_ref.1) | copy-start | bytes 393220
  3.2 0.9 %copy-start.2 = (f32[8,4096]{1,0:T(8,128)S(1)}, f32[8,4096]{1,0:T(8,128)}, u32[]{:S(2)}) copy-start(f32[8,4096]{1,0:T(8,128)} %p_ref.1) | copy-start | bytes 393220

commit v2 on v1

--- a/solution.py
+++ b/solution.py
@@ -39,12 +39,6 @@
 
 def padded(a):
     return jnp.concatenate([a, jnp.zeros((B - a.shape[0], a.shape[1]), F32)], 0)
-
-
-def transposed(a):
-    n = a.shape[0]
-    unit = (lane_ids((n, n)) == row_ids((n, n))).astype(F32)
-    return nt(unit, a[:, :n])
 
 
 def packed(a):
@@ -71,8 +65,8 @@
 
 
 def kernel(rows_ref, cols_ref, h_ref, x_ref, p_ref, q_ref, ray_ref,
-           h, x, x_far, p, p_far, d, m, got_d, got_m, piece, y, y_far, mine, buf_a, buf_b,
-           load_sem, x_sem, p_sem, xs_sem, ps_sem, d_sem, m_sem, ds_sem, ms_sem,
+           rows, cols, h, x, x_far, p, p_far, p_pick, asked, wanted, d, m, got_d, got_m, piece, y, y_far, mine, buf_a, buf_b,
+           load_sem, x_sem, p_sem, want_sem, wants_sem, xs_sem, ps_sem, d_sem, m_sem, ds_sem, ms_sem,
            y_sem, yfar_sem, ys_sem, yfs_sem, a_sem, b_sem, as_sem, bs_sem, step2, step3):
     r, c = lax.axis_index("row"), lax.axis_index("col")
     z, y_lo, l, y_hi = rem(r, Z), div(r, Z), rem(c, L), div(c, L)
@@ -116,9 +110,10 @@
     greet(Y, barrier, lambda k: at(rem(yy + k, Y), z, l))
     greet(L, barrier, lambda k: at(yy, z, rem(l + k, L)))
 
-    pltpu.make_async_copy(h_ref, h, load_sem.at[0]).start()
-    pltpu.make_async_copy(x_ref, x, load_sem.at[1]).start()
-    pltpu.make_async_copy(p_ref, p, load_sem.at[2]).start()
+    loads = [pltpu.make_async_copy(src, dst, load_sem.at[i]) for i, (src, dst) in enumerate(
+        ((rows_ref, rows), (cols_ref, cols), (x_ref, x), (h_ref, h), (p_ref, p)))]
+    for load in loads:
+        load.start()
 
     users_here = users[0][0].astype(jnp.int32) + users[1][0].astype(jnp.int32)
     pl.semaphore_wait(barrier, Z - 1 + Y - 1 + L - 1 + users_here)
@@ -131,14 +126,12 @@
     @pl.when(jnp.logical_not(reads))
     def _():
         pltpu.make_async_copy(x_ref, x_far, x_sem).start()
-        pltpu.make_async_copy(p_ref, p_far, p_sem).start()
 
     greet(Y, step2, lambda k: at(rem(yy + k, Y), z, l))
     pl.semaphore_wait(step2, Y - 1)
     greet(Z, step3, lambda k: at(yy, rem(z + k, Z), l))
-    pltpu.make_async_copy(h_ref, h, load_sem.at[0]).wait()
-    pltpu.make_async_copy(x_ref, x, load_sem.at[1]).wait()
-    pltpu.make_async_copy(p_ref, p, load_sem.at[2]).wait()
+    for load in loads:
+        load.wait()
 
     def blocks(ref, places):
         found = [ref[:, :B]] * NB
@@ -154,43 +147,51 @@
                 total = total + jnp.where(places[n] == b, terms[n], 0.0)
             out[:, b * B : (b + 1) * B] = total
 
-    row_at = [jnp.full((K, B), rows_ref[n], jnp.int32) for n in range(NB)]
-    col_at = [jnp.full((K, B), cols_ref[n], jnp.int32) for n in range(NB)]
+    row_at = [jnp.full((K, B), rows[n], jnp.int32) for n in range(NB)]
+    col_at = [jnp.full((K, B), cols[n], jnp.int32) for n in range(NB)]
     x_row, p_row = blocks(x, row_at), blocks(p, row_at)
     both = [nn(jnp.concatenate([x_row[n], p_row[n]], 0), h[n]) for n in range(NB)]
     spread([both[n][:K] for n in range(NB)], col_at, m)
 
     pl.semaphore_wait(step3, Z - 1)
 
-    def send_m(k, carry):
-        j = rem(c + k, N_COL)
+    asks = jnp.zeros((8, B), jnp.int32)
+    for n in range(NB):
+        asks = jnp.where(row_ids((8, B)) == n, col_at[n], asks)
+    asked[...] = asks
+
+    @pl.when(reads)
+    def _():
+        for hi in range(YH):
+            @pl.when(y_hi == hi)
+            def _(hi=hi):
+                send(asked, wanted.at[hi], wants_sem, want_sem.at[hi], source)
+
+    near_last = (4, 5, 3, 6, 2, 7, 1, 0)
+    for k in range(N_COL):
+        j = rem(rem(y_hi + 1 + k // L, YH) * L + rem(l + near_last[k % L], L), N_COL)
         src, dst = m.at[:, pl.ds(pl.multiple_of(j * SHARE, SHARE), SHARE)], got_m.at[c]
-        local = jnp.logical_and(c == 0, k == 0)
-
-        @pl.when(local)
-        def _():
-            pltpu.make_async_copy(src, dst, m_sem).start()
-
-        @pl.when(jnp.logical_not(local))
-        def _():
+        if k < N_COL - 1:
             send(src, dst, ms_sem, m_sem, (q, j))
-        return carry
-
-    lax.fori_loop(0, N_COL, send_m, 0)
+        else:
+            @pl.when(reads)
+            def _(src=src, dst=dst, j=j):
+                send(src, dst, ms_sem, m_sem, (q, j))
+
+            @pl.when(jnp.logical_not(reads))
+            def _(src=src, dst=dst):
+                pltpu.make_async_copy(src, dst, m_sem).start()
 
     done(x_far, x_sem)
     x_col = blocks(x_far, col_at)
     direct = [nt(x_col[n], h[n]) for n in range(NB)]
     spread(direct, row_at, d)
 
-    def send_d(k, carry):
-        j = rem(c + k, N_COL)
+    own = pl.ds(pl.multiple_of(c * SHARE, SHARE), SHARE)
+    for k in range(N_COL - 1):
+        j = rem(y_hi + 1 + k // L, YH) * L + rem(l + near_last[k % L], L)
         send(d.at[:, pl.ds(pl.multiple_of(j * SHARE, SHARE), SHARE)], got_d.at[c], ds_sem, d_sem, (r, j))
-        return carry
-
-    own = pl.ds(pl.multiple_of(c * SHARE, SHARE), SHARE)
     pltpu.make_async_copy(d.at[:, own], got_d.at[c], d_sem).start()
-    lax.fori_loop(1, N_COL, send_d, 0)
 
     y_par, y_pair = rem(yy, 2), div(yy, 2)
     slot_a = y_par * L + l
@@ -198,13 +199,10 @@
 
     def first(i, tile):
         mine[i, 0] = tile
+        for k in range(2 * L - 1):
+            y_to = 2 * y_pair + rem(y_par + 1 + k // L, 2)
+            send(mine.at[i, 0], buf_a.at[i, slot_a], as_sem.at[i], a_sem.at[i], at(y_to, z, rem(l + near_last[k % L], L)))
         pltpu.make_async_copy(mine.at[i, 0], buf_a.at[i, slot_a], a_sem.at[i]).start()
-
-        def one(k, carry):
-            y_to = 2 * y_pair + rem(y_par + div(k, L), 2)
-            send(mine.at[i, 0], buf_a.at[i, slot_a], as_sem.at[i], a_sem.at[i], at(y_to, z, rem(l + k, L)))
-            return carry
-        lax.fori_loop(1, 2 * L, one, 0)
 
     def second(i):
         done(buf_a.at[i], a_sem.at[i])
@@ -212,13 +210,12 @@
         for s in range(1, 2 * L):
             total = total + buf_a[i, s]
         mine[i, 1] = total
+        for y_k in (2, 1, 3, 0):
+            for z_k in near_last:
+                if y_k or z_k:
+                    y_to = 2 * rem(y_pair + y_k, Y // 2) + y_par
+                    send(mine.at[i, 1], buf_b.at[i, slot_b], bs_sem.at[i], b_sem.at[i], at(y_to, rem(z + z_k, Z), l))
         pltpu.make_async_copy(mine.at[i, 1], buf_b.at[i, slot_b], b_sem.at[i]).start()
-
-        def one(k, carry):
-            y_to = 2 * rem(y_pair + div(k, Z), Y // 2) + y_par
-            send(mine.at[i, 1], buf_b.at[i, slot_b], bs_sem.at[i], b_sem.at[i], at(y_to, rem(z + k, Z), l))
-            return carry
-        lax.fori_loop(1, Z * Y // 2, one, 0)
 
     def third(i):
         done(buf_b.at[i], b_sem.at[i])
@@ -230,12 +227,20 @@
     m_x = jnp.concatenate([both[n][:K] for n in range(NB)], 1)
     m_p = jnp.concatenate([both[n][K:] for n in range(NB)], 1)
     xc = jnp.concatenate(x_col, 1)
-    first(0, nt(m_x, padded(xc)))
+    first(0, nt(m_x, padded(xc)) + nt(xc, padded(m_x)))
 
     for i, (here, place) in enumerate(users):
         @pl.when(here)
         def _(i=i, place=place):
-            send(p_ref, p_far, ps_sem.at[i], p_sem, place)
+            done(wanted.at[i], want_sem.at[i])
+            asks = wanted[i]
+            found = blocks(p, [jnp.broadcast_to(asks[n : n + 1], (K, B)) for n in range(NB)])
+            p_pick[i] = jnp.concatenate(found, 1)
+            send(p_pick.at[i], p_far, ps_sem.at[i], p_sem, place)
+
+    @pl.when(jnp.logical_not(reads))
+    def _():
+        p_far[...] = jnp.concatenate(blocks(p, col_at), 1)
 
     second(0)
 
@@ -247,35 +252,38 @@
     for s in range(N_COL):
         total = total + got_m[s]
     piece[...] = total
+    for k in range(N_COL):
+        hi, l_to = rem(y_hi + 1 + k // L, YH), near_last[k % L]
+        to = hi * L + l_to
+        place = (rem(r + N_ROW - to, N_ROW), to)
+        if l_to:
+            send(piece, y_far.at[:, own], yfs_sem, yfar_sem, place)
+        else:
+            local = jnp.logical_and(c == 0, to == 0)
+
+            @pl.when(local)
+            def _():
+                pltpu.make_async_copy(piece, y_far.at[:, own], yfar_sem).start()
+
+            @pl.when(jnp.logical_not(local))
+            def _(place=place):
+                send(piece, y_far.at[:, own], yfs_sem, yfar_sem, place)
+
+        if k < N_COL - 1:
+            send(piece, y.at[:, own], ys_sem, y_sem, (r, hi * L + rem(l + l_to, L)))
     pltpu.make_async_copy(piece, y.at[:, own], y_sem).start()
 
-    def send_y(k, carry):
-        local = jnp.logical_and(c == 0, k == 0)
-
-        @pl.when(local)
-        def _():
-            pltpu.make_async_copy(piece, y_far.at[:, own], yfar_sem).start()
-
-        @pl.when(jnp.logical_not(local))
-        def _():
-            send(piece, y_far.at[:, own], yfs_sem, yfar_sem, (rem(r + N_ROW - k, N_ROW), k))
-
-        @pl.when(k != 0)
-        def _():
-            send(piece, y.at[:, own], ys_sem, y_sem, (r, rem(c + k, N_COL)))
-        return carry
-
-    lax.fori_loop(0, N_COL, send_y, 0)
-
-    cross = third(0)[:, :K]
-    theta = (cross + transposed(cross)) / ROWS
+    theta = third(0)[:, :K] / ROWS
     x_own, p_own = x[:, own], p[:, own]
     taken = nn(theta, jnp.concatenate(x_row + x_col + [x_own], 1))
     basis = jnp.concatenate([total - taken[:, 2 * NB * B :], x_own, p_own], 0)
     first(1, packed(nt(basis, padded(basis))))
 
-    done(p_far, p_sem)
-    p_col = jnp.concatenate(blocks(p_far, col_at), 1)
+    @pl.when(reads)
+    def _():
+        done(p_far, p_sem)
+
+    p_col = p_far[...]
     second(1)
 
     done(y, y_sem)
@@ -284,52 +292,76 @@
 
     done(y_far, yfar_sem)
     r_col = jnp.concatenate(blocks(y_far, col_at), 1) - taken[:, NB * B : 2 * NB * B]
-    first(2, packed(nt(jnp.concatenate([m_r, m_x, m_p], 0), padded(jnp.concatenate([r_col, xc, p_col], 0)))))
+    left, right = jnp.concatenate([m_r, m_x, m_p], 0), jnp.concatenate([r_col, xc, p_col], 0)
+    first(2, packed(nt(left, padded(right)) + nt(right, padded(left))))
     second(2)
 
     inverse = inverse_factor(unpacked(third(1)) / ROWS)[:, :24]
     q_ref[...] = nn(inverse, basis)
-
-    half = unpacked(third(2))[:, :24]
-    ray_ref[...] = nt(nn(inverse, (half + transposed(half)) / ROWS), inverse)
 
     for i, (here, place) in enumerate(users):
         @pl.when(here)
         def _(i=i):
             done(x_ref, xs_sem.at[i])
-            done(p_ref, ps_sem.at[i])
+
+    @pl.when(reads)
+    def _():
+        done(asked, wants_sem)
+
+    for i, (here, place) in enumerate(users):
+        @pl.when(here)
+        def _(i=i):
+            done(p_pick.at[i], ps_sem.at[i])
 
     @pl.when(reads)
     def _():
         done(got_m, ms_sem)
+
+    @pl.when(jnp.logical_not(reads))
+    def _():
+        done(got_m.at[pl.ds(0, N_COL - 1)], ms_sem)
+
+    @pl.when(reads)
+    def _():
         done(got_m, yfs_sem)
 
     @pl.when(jnp.logical_not(reads))
     def _():
-        done(got_m.at[pl.ds(0, N_COL - 1)], ms_sem)
         done(got_m.at[pl.ds(0, N_COL - 1)], yfs_sem)
 
+    done(got_d.at[pl.ds(0, N_COL - 1)], ys_sem)
+
     done(got_d.at[pl.ds(0, N_COL - 1)], ds_sem)
-    done(got_d.at[pl.ds(0, N_COL - 1)], ys_sem)
-    for i in range(3):
-        done(buf_a.at[i, pl.ds(0, 2 * L - 1)], as_sem.at[i])
-        done(buf_b.at[i, pl.ds(0, Z * Y // 2 - 1)], bs_sem.at[i])
+
+    done(buf_a.at[0, pl.ds(0, 2 * L - 1)], as_sem.at[0])
+    done(buf_b.at[0, pl.ds(0, Z * Y // 2 - 1)], bs_sem.at[0])
+    done(buf_a.at[1, pl.ds(0, 2 * L - 1)], as_sem.at[1])
+    done(buf_b.at[1, pl.ds(0, Z * Y // 2 - 1)], bs_sem.at[1])
+    done(buf_a.at[2, pl.ds(0, 2 * L - 1)], as_sem.at[2])
+
+    ray_ref[...] = nt(nn(inverse, unpacked(third(2))[:, :24] / ROWS), inverse)
+    done(buf_b.at[2, pl.ds(0, Z * Y // 2 - 1)], bs_sem.at[2])
 
 
 def body(hamiltonian_blocks, block_rows, block_cols, current_states, previous_steps):
-    vmem, smem, anywhere = (pl.BlockSpec(memory_space=s) for s in (pltpu.VMEM, pltpu.SMEM, pl.ANY))
+    vmem, anywhere = (pl.BlockSpec(memory_space=s) for s in (pltpu.VMEM, pl.ANY))
     dma, regular = pltpu.SemaphoreType.DMA, pltpu.SemaphoreType.REGULAR
     return pl.pallas_call(
         kernel,
         out_shape=(jax.ShapeDtypeStruct((3 * K, SHARE), F32), jax.ShapeDtypeStruct((3 * K, 3 * K), F32)),
-        in_specs=[smem, smem, anywhere, anywhere, anywhere],
+        in_specs=[anywhere, anywhere, anywhere, anywhere, anywhere],
         out_specs=(vmem, vmem),
         scratch_shapes=[
+            pltpu.SMEM((NB,), jnp.int32),
+            pltpu.SMEM((NB,), jnp.int32),
             pltpu.VMEM((NB, B, B), F32),
             pltpu.VMEM((K, SEG), F32),
             pltpu.VMEM((K, SEG), F32),
             pltpu.VMEM((K, SEG), F32),
-            pltpu.VMEM((K, SEG), F32),
+            pltpu.VMEM((K, NB * B), F32),
+            pltpu.VMEM((YH, K, NB * B), F32),
+            pltpu.VMEM((8, B), jnp.int32),
+            pltpu.VMEM((YH, 8, B), jnp.int32),
             pltpu.VMEM((K, SEG), F32),
             pltpu.VMEM((K, SEG), F32),
             pltpu.VMEM((N_COL, K, SHARE), F32),
@@ -340,10 +372,10 @@
             pltpu.VMEM((3, 2, 8, B), F32),
             pltpu.VMEM((3, 2 * L, 8, B), F32),
             pltpu.VMEM((3, Z * Y // 2, 8, B), F32),
-            dma((3,)), dma, dma, dma((2,)), dma((2,)), dma, dma, dma, dma,
+            dma((5,)), dma, dma, dma((YH,)), dma, dma((2,)), dma((2,)), dma, dma, dma, dma,
             dma, dma, dma, dma, dma((3,)), dma((3,)), dma((3,)), dma((3,)), regular, regular,
         ],
-        compiler_params=pltpu.CompilerParams(collective_id=0, has_side_effects=True, vmem_limit_bytes=32 * 1024 * 1024),
+        compiler_params=pltpu.CompilerParams(collective_id=0, has_side_effects=True, vmem_limit_bytes=62 * 1024 * 1024),
         name="lobpcg_step",
     )(block_rows.reshape(NB), block_cols.reshape(NB), hamiltonian_blocks.reshape(NB, B, B), current_states, previous_steps)
 

time: 75.9 us -> 71.3 us (0.939)
  local copies, waits for them, and re-layouts: 4.62 us -> 1.96 us
  Pallas kernels: 70.4 us -> 68.5 us
    unnamed x12 -> x4, local copies, waits for them, and re-layouts: 4.62 us -> 1.96 us
    pallas_call x1, Pallas kernels: 70.4 us -> 68.5 us  [body(): pl.pallas_call(kernel, out_shape=(jax.ShapeDtypeStruct((3 * K, SHARE), F3...]
where the time goes in v2:
time: 71.3 us; the launch traced here: 71.1 us
  Pallas kernels  68.5 us (96%)
  local copies, waits for them, and re-layouts  1.96 us (3%)
    pallas_call x1, Pallas kernels, body(): pl.pallas_call(kernel, out_shape=(jax.ShapeDtypeStruct((3 * K, SHARE), F3...  68.5 us
    unnamed x4, local copies, waits for them, and re-layouts  1.96 us

profile of v2, /device:TPU:1, one launch (start us, length us, event | category | flops | bytes accessed | tf_op | source)
XLA Modules:
  0.0 71.1 jit_solution(11880074422068398501)
XLA Ops:
  0.6 68.5 %lobpcg_step.1 = (f32[24,256]{1,0:T(8,128)}, f32[24,24]{1,0:T(8,128)}) custom-call(s32[4]{0:T(128)} %bitcast.4, s32[4]{0:T(128)} %bitcast.5, f32[4,128,128]{2,1,0:T(8,128)} %bitcast.3, f32[8,4096]{1,0:T(8,128)} %x_ref.1, f32[8,4096]{1,0:T(8,128)} %p_ref.1), custom_call_target="tpu_custom_call" | custom-call | tf_op jit(solution)/shard_map/lobpcg_step/pallas_call | solution.py:349
  69.2 0.0 copy-start
  69.2 1.4 %copy.9 = f32[24,256]{1,0:T(8,128)} copy(f32[24,256]{1,0:T(8,128)} %get-tuple-element.4) | data formatting | bytes 49152
  70.5 0.0 copy-done
  70.5 0.6 copy.10
Async XLA Ops:
  69.2 1.4 %copy-start = (f32[24,24]{1,0:T(8,128)S(1)}, f32[24,24]{1,0:T(8,128)}, u32[]{:S(2)}) copy-start(f32[24,24]{1,0:T(8,128)} %get-tuple-element.5) | copy-start | bytes 6916

commit v3 on v2

v3 whole, which is shorter than its diff:
```python
import functools

import jax
import jax.numpy as jnp
from jax import lax
from jax.experimental import pallas as pl
from jax.experimental.pallas import tpu as pltpu
from jax.sharding import PartitionSpec as P

MESH = pl.DeviceIdType.MESH
F32 = jnp.float32
exactness = lax.Precision.HIGHEST

Z, YL, YH, L = 8, 4, 2, 8
Y = YL * YH
N_ROW, N_COL = Z * YL, L * YH
K, B, SEGB, NB = 8, 128, 32, 4
SEG = SEGB * B
SHARE, OWNED = SEG // N_COL, SEG // L
ROWS = N_ROW * SEG
rem, div = lax.rem, lax.div


def nn(a, b):
    return jnp.dot(a, b, precision=exactness, preferred_element_type=F32)


def nt(a, b):
    return lax.dot_general(a, b, (((1,), (1,)), ((), ())), precision=exactness, preferred_element_type=F32)


def lane_ids(shape):
    return lax.broadcasted_iota(jnp.int32, shape, 1)


def row_ids(shape):
    return lax.broadcasted_iota(jnp.int32, shape, 0)


def padded(a):
    return jnp.concatenate([a, jnp.zeros((B - a.shape[0], a.shape[1]), F32)], 0)


def packed(a):
    return a[0:8] + pltpu.roll(a[8:16], 32, 1) + pltpu.roll(a[16:24], 64, 1)


def unpacked(t):
    a = jnp.concatenate([t, pltpu.roll(t, 96, 1), pltpu.roll(t, 64, 1)], 0)
    return jnp.where(lane_ids(a.shape) < 24, a, 0.0)


def inverse_factor(gram):
    rows, lanes = row_ids(gram.shape), lane_ids(gram.shape)
    left = gram
    right = (rows == lanes).astype(F32)
    for j in range(24):
        pivot = left[j : j + 1, j : j + 1]
        factor = jnp.where(rows[:, :1] > j, left[:, j : j + 1] / pivot, 0.0)
        top, unit = left[j : j + 1], right[j : j + 1]
        left = left - factor * top
        right = right - factor * unit
    diagonal = jnp.sum(jnp.where(rows == lanes, left, 0.0), 1, keepdims=True)
    return right / jnp.sqrt(diagonal)


def kernel(rows_ref, cols_ref, h_ref, x_ref, p_ref, q_ref, ray_ref,
           rows, cols, h, x, x_far, p, p_far, p_pick, asked, wanted, m, m_near, d, got, part, other, piece, y, y_far, mine,
           buf_a, buf_b, load_sem, x_sem, xs_sem, m_sem, ms_sem, want_sem, wants_sem, p_sem, ps_sem, d_sem, ds_sem, o_sem, os_sem,
           y_sem, ys_sem, yfar_sem, yfs_sem, a_sem, b_sem, as_sem, bs_sem, step2, step3):
    r, c = lax.axis_index("row"), lax.axis_index("col")
    z, y_lo, l, y_hi = rem(r, Z), div(r, Z), rem(c, L), div(c, L)
    yy = y_hi * YL + y_lo

    def at(y_at, z_at, l_at):
        return (rem(y_at, YL) * Z + z_at, div(y_at, YL) * L + l_at)

    def send(src, dst, ss, rs, dev):
        pltpu.make_async_remote_copy(src_ref=src, dst_ref=dst, send_sem=ss, recv_sem=rs,
                                     device_id=dev, device_id_type=MESH).start()

    def done(ref, sem):
        pltpu.make_async_copy(ref, ref, sem).wait()

    reads = c != 0
    q = rem(r + c, N_ROW)
    turned = jnp.logical_and(div(q, Z) == 0, z + l >= Z).astype(jnp.int32)
    source = (q, rem(y_hi + turned, YH) * L + l)

    def user(l_at):
        over = jnp.logical_and(y_lo == 0, z < l_at).astype(jnp.int32)
        to = rem(y_hi + over, YH) * L + l_at
        return rem(r + N_ROW - to, N_ROW), to

    barrier = pltpu.get_barrier_semaphore()

    @pl.when(reads)
    def _():
        pl.semaphore_signal(barrier, inc=1, device_id=source, device_id_type=MESH)
        pl.semaphore_signal(barrier, inc=1, device_id=user(l), device_id_type=MESH)

    def greet(n, sem, place):
        for k in range(1, n):
            pl.semaphore_signal(sem, inc=1, device_id=place(k), device_id_type=MESH)

    greet(Z, barrier, lambda k: at(yy, rem(z + k, Z), l))
    greet(Y, barrier, lambda k: at(rem(yy + k, Y), z, l))
    greet(L, barrier, lambda k: at(yy, z, rem(l + k, L)))

    loads = [pltpu.make_async_copy(src, dst, load_sem.at[i]) for i, (src, dst) in enumerate(
        ((rows_ref, rows), (cols_ref, cols), (x_ref, x), (h_ref, h), (p_ref, p)))]
    for load in loads:
        load.start()

    pl.semaphore_wait(barrier, Z - 1 + Y - 1 + L - 1 + 2 * reads.astype(jnp.int32))

    @pl.when(reads)
    def _():
        send(x_ref, x_far, xs_sem, x_sem, user(l))

    @pl.when(jnp.logical_not(reads))
    def _():
        pltpu.make_async_copy(x_ref, x_far, x_sem).start()

    greet(Y, step2, lambda k: at(rem(yy + k, Y), z, l))

    def blocks(ref, places):
        found = [ref[:, :B]] * NB
        for b in range(1, SEGB):
            here = ref[:, b * B : (b + 1) * B]
            found = [jnp.where(places[n] == b, here, found[n]) for n in range(NB)]
        return found

    for load in loads[:4]:
        load.wait()
    row_at = [jnp.full((K, B), rows[n], jnp.int32) for n in range(NB)]
    col_at = [jnp.full((K, B), cols[n], jnp.int32) for n in range(NB)]
    x_row = blocks(x, row_at)
    m_x = jnp.concatenate([nn(x_row[n], h[n]) for n in range(NB)], 1)

    asks = jnp.zeros((8, B), jnp.int32)
    for n in range(NB):
        asks = jnp.where(row_ids((8, B)) == n, col_at[n], asks)

    @pl.when(reads)
    def _():
        m[...] = m_x
        asked[...] = asks
        send(m, m_near, ms_sem, m_sem, source)
        send(asked, wanted, wants_sem, want_sem, source)

    @pl.when(jnp.logical_not(reads))
    def _():
        m_near[...] = m_x
        wanted[...] = asks

    pl.semaphore_wait(step2, Y - 1)
    greet(Z, step3, lambda k: at(yy, rem(z + k, Z), l))
    loads[4].wait()
    p_row = blocks(p, row_at)
    m_p = jnp.concatenate([nn(p_row[n], h[n]) for n in range(NB)], 1)

    done(x_far, x_sem)
    x_col = blocks(x_far, col_at)
    direct = [nt(x_col[n], h[n]) for n in range(NB)]
    xc = jnp.concatenate(x_col, 1)

    @pl.when(reads)
    def _():
        done(m_near, m_sem)
        done(wanted, want_sem)

    want = wanted[...]
    want_at = [jnp.broadcast_to(want[n : n + 1], (K, B)) for n in range(NB)]
    terms = [direct[n] for n in range(NB)] + [m_near[:, n * B : (n + 1) * B] for n in range(NB)]
    for b in range(SEGB):
        total = jnp.zeros((K, B), F32)
        for place, term in zip(row_at + want_at, terms):
            total = total + jnp.where(place == b, term, 0.0)
        d[:, b * B : (b + 1) * B] = total
    pl.semaphore_wait(step3, Z - 1)

    near_last = (4, 5, 3, 6, 2, 7, 1, 0)

    def share(l_at):
        return pl.ds(pl.multiple_of(l_at * OWNED, OWNED), OWNED)

    for k in near_last[:-1]:
        j = rem(l + k, L)
        send(d.at[:, share(j)], got.at[l], ds_sem, d_sem, at(yy, z, j))
    pltpu.make_async_copy(d.at[:, share(l)], got.at[l], d_sem).start()

    y_par, y_pair = rem(yy, 2), div(yy, 2)
    slot_a = y_par * L + l
    slot_b = y_pair * Z + z

    def first(i, tile):
        mine[i, 0] = tile
        for k in range(2 * L - 1):
            y_to = 2 * y_pair + rem(y_par + 1 + k // L, 2)
            send(mine.at[i, 0], buf_a.at[i, slot_a], as_sem.at[i], a_sem.at[i], at(y_to, z, rem(l + near_last[k % L], L)))
        pltpu.make_async_copy(mine.at[i, 0], buf_a.at[i, slot_a], a_sem.at[i]).start()

    def second(i):
        done(buf_a.at[i], a_sem.at[i])
        total = buf_a[i, 0]
        for s in range(1, 2 * L):
            total = total + buf_a[i, s]
        mine[i, 1] = total
        for y_k in (2, 1, 3, 0):
            for z_k in near_last:
                if y_k or z_k:
                    y_to = 2 * rem(y_pair + y_k, Y // 2) + y_par
                    send(mine.at[i, 1], buf_b.at[i, slot_b], bs_sem.at[i], b_sem.at[i], at(y_to, rem(z + z_k, Z), l))
        pltpu.make_async_copy(mine.at[i, 1], buf_b.at[i, slot_b], b_sem.at[i]).start()

    def third(i):
        done(buf_b.at[i], b_sem.at[i])
        total = buf_b[i, 0]
        for s in range(1, Z * Y // 2):
            total = total + buf_b[i, s]
        return total

    first(0, nt(m_x, padded(xc)) + nt(xc, padded(m_x)))

    @pl.when(reads)
    def _():
        p_pick[...] = jnp.concatenate(blocks(p, want_at), 1)
        send(p_pick, p_far, ps_sem, p_sem, user(l))

    @pl.when(jnp.logical_not(reads))
    def _():
        p_far[...] = jnp.concatenate(blocks(p, col_at), 1)

    done(got, d_sem)
    total = got[0]
    for s in range(1, L):
        total = total + got[s]
    part[...] = total
    send(part, other, os_sem, o_sem, (r, rem(y_hi + 1, YH) * L + l))
    second(0)
    done(other, o_sem)
    total = part[...] + other[...]
    piece[...] = total

    mine_of = share(l)
    for l_to in near_last:
        if l_to:
            send(piece, y_far.at[:, mine_of], yfs_sem, yfar_sem, user(l_to))
        else:
            @pl.when(c == 0)
            def _():
                pltpu.make_async_copy(piece, y_far.at[:, mine_of], yfar_sem).start()

            @pl.when(reads)
            def _():
                send(piece, y_far.at[:, mine_of], yfs_sem, yfar_sem, user(0))

    for k in near_last[:-1]:
        send(piece, y.at[:, mine_of], ys_sem, y_sem, at(yy, z, rem(l + k, L)))
    pltpu.make_async_copy(piece, y.at[:, mine_of], y_sem).start()

    theta = third(0)[:, :K] / ROWS
    half = pl.ds(pl.multiple_of(l * OWNED + y_hi * SHARE, SHARE), SHARE)
    half_of = pl.ds(pl.multiple_of(y_hi * SHARE, SHARE), SHARE)
    own = pl.ds(pl.multiple_of(c * SHARE, SHARE), SHARE)
    taken = nn(theta, jnp.concatenate(x_row + x_col + [x[:, half], x[:, own]], 1))
    basis = jnp.concatenate([piece[:, half_of] - taken[:, 2 * NB * B : 2 * NB * B + SHARE], x[:, half], p[:, half]], 0)
    first(1, packed(nt(basis, padded(basis))))

    @pl.when(reads)
    def _():
        done(p_far, p_sem)

    p_col = p_far[...]
    done(y, y_sem)
    y_row = blocks(y, row_at)
    m_r = jnp.concatenate([nn(y_row[n] - taken[:, n * B : (n + 1) * B], h[n]) for n in range(NB)], 1)

    done(y_far, yfar_sem)
    r_col = jnp.concatenate(blocks(y_far, col_at), 1) - taken[:, NB * B : 2 * NB * B]
    left, right = jnp.concatenate([m_r, m_x, m_p], 0), jnp.concatenate([r_col, xc, p_col], 0)
    first(2, packed(nt(left, padded(right)) + nt(right, padded(left))))
    second(1)
    second(2)
    inverse = inverse_factor(unpacked(third(1)) / ROWS)[:, :24]
    q_ref[...] = nn(inverse, jnp.concatenate([y[:, own] - taken[:, 2 * NB * B + SHARE :], x[:, own], p[:, own]], 0))

    @pl.when(reads)
    def _():
        done(x_ref, xs_sem)

    @pl.when(reads)
    def _():
        done(m, ms_sem)
        done(asked, wants_sem)

    @pl.when(reads)
    def _():
        done(p_pick, ps_sem)

    done(got.at[pl.ds(0, L - 1)], ds_sem)
    done(part, os_sem)
    done(got.at[pl.ds(0, L - 1)], yfs_sem)
    done(got.at[pl.ds(0, L - 1)], ys_sem)

    @pl.when(reads)
    def _():
        done(piece, yfs_sem)

    done(buf_a.at[0, pl.ds(0, 2 * L - 1)], as_sem.at[0])
    done(buf_b.at[0, pl.ds(0, Z * Y // 2 - 1)], bs_sem.at[0])
    done(buf_a.at[1, pl.ds(0, 2 * L - 1)], as_sem.at[1])
    done(buf_b.at[1, pl.ds(0, Z * Y // 2 - 1)], bs_sem.at[1])
    done(buf_a.at[2, pl.ds(0, 2 * L - 1)], as_sem.at[2])

    ray_ref[...] = nt(nn(inverse, unpacked(third(2))[:, :24] / ROWS), inverse)
    done(buf_b.at[2, pl.ds(0, Z * Y // 2 - 1)], bs_sem.at[2])


def body(hamiltonian_blocks, block_rows, block_cols, current_states, previous_steps):
    vmem, anywhere = (pl.BlockSpec(memory_space=s) for s in (pltpu.VMEM, pl.ANY))
    dma, regular = pltpu.SemaphoreType.DMA, pltpu.SemaphoreType.REGULAR
    return pl.pallas_call(
        kernel,
        out_shape=(jax.ShapeDtypeStruct((3 * K, SHARE), F32), jax.ShapeDtypeStruct((3 * K, 3 * K), F32)),
        in_specs=[anywhere, anywhere, anywhere, anywhere, anywhere],
        out_specs=(vmem, vmem),
        scratch_shapes=[
            pltpu.SMEM((NB,), jnp.int32),
            pltpu.SMEM((NB,), jnp.int32),
            pltpu.VMEM((NB, B, B), F32),
            pltpu.VMEM((K, SEG), F32),
            pltpu.VMEM((K, SEG), F32),
            pltpu.VMEM((K, SEG), F32),
            pltpu.VMEM((K, NB * B), F32),
            pltpu.VMEM((K, NB * B), F32),
            pltpu.VMEM((8, B), jnp.int32),
            pltpu.VMEM((8, B), jnp.int32),
            pltpu.VMEM((K, NB * B), F32),
            pltpu.VMEM((K, NB * B), F32),
            pltpu.VMEM((K, SEG), F32),
            pltpu.VMEM((L, K, OWNED), F32),
            pltpu.VMEM((K, OWNED), F32),
            pltpu.VMEM((K, OWNED), F32),
            pltpu.VMEM((K, OWNED), F32),
            pltpu.VMEM((K, SEG), F32),
            pltpu.VMEM((K, SEG), F32),
            pltpu.VMEM((3, 2, 8, B), F32),
            pltpu.VMEM((3, 2 * L, 8, B), F32),
            pltpu.VMEM((3, Z * Y // 2, 8, B), F32),
            dma((5,)), dma, dma, dma, dma, dma, dma, dma, dma, dma, dma, dma, dma,
            dma, dma, dma, dma, dma((3,)), dma((3,)), dma((3,)), dma((3,)), regular, regular,
        ],
        compiler_params=pltpu.CompilerParams(collective_id=0, has_side_effects=True, vmem_limit_bytes=62 * 1024 * 1024),
        name="lobpcg_step",
    )(block_rows.reshape(NB), block_cols.reshape(NB), hamiltonian_blocks.reshape(NB, B, B), current_states, previous_steps)


def solution(mesh):
    return jax.shard_map(
        body,
        mesh=mesh,
        in_specs=(
            P("row", "col", None, None, None),
            P("row", "col", None),
            P("row", "col", None),
            P(None, "row"),
            P(None, "row"),
        ),
        out_specs=(P(None, ("row", "col")), P()),
        check_vma=False,
    )
```

time: 71.3 us -> 62.2 us (0.87)
  Pallas kernels: 68.5 us -> 59.4 us
    pallas_call x1, Pallas kernels: 68.5 us -> 59.4 us  [body(): pl.pallas_call(kernel, out_shape=(jax.ShapeDtypeStruct((3 * K, SHARE), F3...]
where the time goes in v3:
time: 62.2 us; the launch traced here: 62 us
  Pallas kernels  59.4 us (95%)
  local copies, waits for them, and re-layouts  1.96 us (3%)
  between operations  0.65 us (1%)
    pallas_call x1, Pallas kernels, body(): pl.pallas_call(kernel, out_shape=(jax.ShapeDtypeStruct((3 * K, SHARE), F3...  59.4 us
    unnamed x4, local copies, waits for them, and re-layouts  1.96 us

profile of v3, /device:TPU:1, one launch (start us, length us, event | category | flops | bytes accessed | tf_op | source)
XLA Modules:
  0.0 62.0 jit_solution(5262552011461264679)
XLA Ops:
  0.6 59.4 %lobpcg_step.1 = (f32[24,256]{1,0:T(8,128)}, f32[24,24]{1,0:T(8,128)}) custom-call(s32[4]{0:T(128)} %bitcast.4, s32[4]{0:T(128)} %bitcast.5, f32[4,128,128]{2,1,0:T(8,128)} %bitcast.3, f32[8,4096]{1,0:T(8,128)} %x_ref.1, f32[8,4096]{1,0:T(8,128)} %p_ref.1), custom_call_target="tpu_custom_call" | custom-call | tf_op jit(solution)/shard_map/lobpcg_step/pallas_call | solution.py:324
  60.1 0.0 copy-start
  60.1 1.4 %copy.9 = f32[24,256]{1,0:T(8,128)} copy(f32[24,256]{1,0:T(8,128)} %get-tuple-element.4) | data formatting | bytes 49152
  61.4 0.0 copy-done
  61.4 0.6 copy.10
Async XLA Ops:
  60.1 1.4 %copy-start = (f32[24,24]{1,0:T(8,128)S(1)}, f32[24,24]{1,0:T(8,128)}, u32[]{:S(2)}) copy-start(f32[24,24]{1,0:T(8,128)} %get-tuple-element.5) | copy-start | bytes 6916

commit v4 on v3

--- a/solution.py
+++ b/solution.py
@@ -39,6 +39,12 @@
 
 def padded(a):
     return jnp.concatenate([a, jnp.zeros((B - a.shape[0], a.shape[1]), F32)], 0)
+
+
+def summed(terms):
+    while len(terms) > 1:
+        terms = [sum(terms[i + 1 : i + 2], terms[i]) for i in range(0, len(terms), 2)]
+    return terms[0]
 
 
 def packed(a):
@@ -66,8 +72,8 @@
 
 def kernel(rows_ref, cols_ref, h_ref, x_ref, p_ref, q_ref, ray_ref,
            rows, cols, h, x, x_far, p, p_far, p_pick, asked, wanted, m, m_near, d, got, part, other, piece, y, y_far, mine,
-           buf_a, buf_b, load_sem, x_sem, xs_sem, m_sem, ms_sem, want_sem, wants_sem, p_sem, ps_sem, d_sem, ds_sem, o_sem, os_sem,
-           y_sem, ys_sem, yfar_sem, yfs_sem, a_sem, b_sem, as_sem, bs_sem, step2, step3):
+           line, buf_a, buf_b, buf_c, load_sem, x_sem, xs_sem, m_sem, ms_sem, want_sem, wants_sem, p_sem, ps_sem, d_sem, ds_sem, o_sem, os_sem,
+           y_sem, ys_sem, yfar_sem, yfs_sem, a_sem, b_sem, c_sem, as_sem, bs_sem, cs_sem, step2, step3):
     r, c = lax.axis_index("row"), lax.axis_index("col")
     z, y_lo, l, y_hi = rem(r, Z), div(r, Z), rem(c, L), div(c, L)
     yy = y_hi * YL + y_lo
@@ -164,6 +170,48 @@
     x_col = blocks(x_far, col_at)
     direct = [nt(x_col[n], h[n]) for n in range(NB)]
     xc = jnp.concatenate(x_col, 1)
+    near_last = (4, 5, 3, 6, 2, 7, 1, 0)
+
+    y_par, y_pair = rem(yy, 2), div(yy, 2)
+    slot_a = y_par * L + l
+    slot_b = y_pair * Z + z
+
+    def first(tile):
+        mine[0] = tile
+        for k in range(2 * L - 1):
+            y_to = 2 * y_pair + rem(y_par + 1 + k // L, 2)
+            send(mine.at[0], buf_a.at[slot_a], as_sem, a_sem, at(y_to, z, rem(l + near_last[k % L], L)))
+        pltpu.make_async_copy(mine.at[0], buf_a.at[slot_a], a_sem).start()
+
+    def second():
+        done(buf_a, a_sem)
+        mine[1] = summed([buf_a[s] for s in range(2 * L)])
+        for y_k in (2, 1, 3, 0):
+            for z_k in near_last:
+                if y_k or z_k:
+                    y_to = 2 * rem(y_pair + y_k, Y // 2) + y_par
+                    send(mine.at[1], buf_b.at[slot_b], bs_sem, b_sem, at(y_to, rem(z + z_k, Z), l))
+        pltpu.make_async_copy(mine.at[1], buf_b.at[slot_b], b_sem).start()
+
+    def third():
+        done(buf_b, b_sem)
+        return summed([buf_b[s] for s in range(Z * Y // 2)])
+
+    def start(i, step, tile):
+        line[i, step] = tile
+        slot = (l, yy, z)[step]
+        for k in near_last[:-1]:
+            to = (at(yy, z, rem(l + k, L)), at(rem(yy + k, Y), z, l), at(yy, rem(z + k, Z), l))[step]
+            send(line.at[i, step], buf_c.at[i, step, slot], cs_sem.at[i, step], c_sem.at[i, step], to)
+        pltpu.make_async_copy(line.at[i, step], buf_c.at[i, step, slot], c_sem.at[i, step]).start()
+
+    def finish(i, step):
+        done(buf_c.at[i, step], c_sem.at[i, step])
+        return summed([buf_c[i, step, s] for s in range(8)])
+
+    pl.semaphore_wait(step3, Z - 1)
+    start(0, 0, nt(m_x, padded(xc)) + nt(xc, padded(m_x)))
+
 
     @pl.when(reads)
     def _():
@@ -178,9 +226,6 @@
         for place, term in zip(row_at + want_at, terms):
             total = total + jnp.where(place == b, term, 0.0)
         d[:, b * B : (b + 1) * B] = total
-    pl.semaphore_wait(step3, Z - 1)
-
-    near_last = (4, 5, 3, 6, 2, 7, 1, 0)
 
     def share(l_at):
         return pl.ds(pl.multiple_of(l_at * OWNED, OWNED), OWNED)
@@ -190,39 +235,6 @@
         send(d.at[:, share(j)], got.at[l], ds_sem, d_sem, at(yy, z, j))
     pltpu.make_async_copy(d.at[:, share(l)], got.at[l], d_sem).start()
 
-    y_par, y_pair = rem(yy, 2), div(yy, 2)
-    slot_a = y_par * L + l
-    slot_b = y_pair * Z + z
-
-    def first(i, tile):
-        mine[i, 0] = tile
-        for k in range(2 * L - 1):
-            y_to = 2 * y_pair + rem(y_par + 1 + k // L, 2)
-            send(mine.at[i, 0], buf_a.at[i, slot_a], as_sem.at[i], a_sem.at[i], at(y_to, z, rem(l + near_last[k % L], L)))
-        pltpu.make_async_copy(mine.at[i, 0], buf_a.at[i, slot_a], a_sem.at[i]).start()
-
-    def second(i):
-        done(buf_a.at[i], a_sem.at[i])
-        total = buf_a[i, 0]
-        for s in range(1, 2 * L):
-            total = total + buf_a[i, s]
-        mine[i, 1] = total
-        for y_k in (2, 1, 3, 0):
-            for z_k in near_last:
-                if y_k or z_k:
-                    y_to = 2 * rem(y_pair + y_k, Y // 2) + y_par
-                    send(mine.at[i, 1], buf_b.at[i, slot_b], bs_sem.at[i], b_sem.at[i], at(y_to, rem(z + z_k, Z), l))
-        pltpu.make_async_copy(mine.at[i, 1], buf_b.at[i, slot_b], b_sem.at[i]).start()
-
-    def third(i):
-        done(buf_b.at[i], b_sem.at[i])
-        total = buf_b[i, 0]
-        for s in range(1, Z * Y // 2):
-            total = total + buf_b[i, s]
-        return total
-
-    first(0, nt(m_x, padded(xc)) + nt(xc, padded(m_x)))
-
     @pl.when(reads)
     def _():
         p_pick[...] = jnp.concatenate(blocks(p, want_at), 1)
@@ -232,16 +244,13 @@
     def _():
         p_far[...] = jnp.concatenate(blocks(p, col_at), 1)
 
+    start(0, 1, finish(0, 0))
     done(got, d_sem)
-    total = got[0]
-    for s in range(1, L):
-        total = total + got[s]
-    part[...] = total
+    part[...] = summed([got[s] for s in range(L)])
     send(part, other, os_sem, o_sem, (r, rem(y_hi + 1, YH) * L + l))
-    second(0)
+    start(0, 2, finish(0, 1))
     done(other, o_sem)
-    total = part[...] + other[...]
-    piece[...] = total
+    piece[...] = part[...] + other[...]
 
     mine_of = share(l)
     for l_to in near_last:
@@ -260,13 +269,14 @@
         send(piece, y.at[:, mine_of], ys_sem, y_sem, at(yy, z, rem(l + k, L)))
     pltpu.make_async_copy(piece, y.at[:, mine_of], y_sem).start()
 
-    theta = third(0)[:, :K] / ROWS
+    theta = finish(0, 2)[:, :K] / ROWS
     half = pl.ds(pl.multiple_of(l * OWNED + y_hi * SHARE, SHARE), SHARE)
     half_of = pl.ds(pl.multiple_of(y_hi * SHARE, SHARE), SHARE)
     own = pl.ds(pl.multiple_of(c * SHARE, SHARE), SHARE)
-    taken = nn(theta, jnp.concatenate(x_row + x_col + [x[:, half], x[:, own]], 1))
-    basis = jnp.concatenate([piece[:, half_of] - taken[:, 2 * NB * B : 2 * NB * B + SHARE], x[:, half], p[:, half]], 0)
-    first(1, packed(nt(basis, padded(basis))))
+    residual = piece[:, half_of] - nn(theta, x[:, half])
+    basis = jnp.concatenate([residual, x[:, half], p[:, half]], 0)
+    start(1, 0, packed(nt(basis, padded(basis))))
+    taken = nn(theta, jnp.concatenate([m_x, xc, x[:, own]], 1))
 
     @pl.when(reads)
     def _():
@@ -275,16 +285,17 @@
     p_col = p_far[...]
     done(y, y_sem)
     y_row = blocks(y, row_at)
-    m_r = jnp.concatenate([nn(y_row[n] - taken[:, n * B : (n + 1) * B], h[n]) for n in range(NB)], 1)
+    m_r = jnp.concatenate([nn(y_row[n], h[n]) for n in range(NB)], 1) - taken[:, : NB * B]
 
     done(y_far, yfar_sem)
     r_col = jnp.concatenate(blocks(y_far, col_at), 1) - taken[:, NB * B : 2 * NB * B]
     left, right = jnp.concatenate([m_r, m_x, m_p], 0), jnp.concatenate([r_col, xc, p_col], 0)
-    first(2, packed(nt(left, padded(right)) + nt(right, padded(left))))
-    second(1)
-    second(2)
-    inverse = inverse_factor(unpacked(third(1)) / ROWS)[:, :24]
-    q_ref[...] = nn(inverse, jnp.concatenate([y[:, own] - taken[:, 2 * NB * B + SHARE :], x[:, own], p[:, own]], 0))
+    first(packed(nt(left, padded(right)) + nt(right, padded(left))))
+    start(1, 1, finish(1, 0))
+    second()
+    start(1, 2, finish(1, 1))
+    inverse = inverse_factor(unpacked(finish(1, 2)) / ROWS)[:, :24]
+    q_ref[...] = nn(inverse, jnp.concatenate([y[:, own] - taken[:, 2 * NB * B :], x[:, own], p[:, own]], 0))
 
     @pl.when(reads)
     def _():
@@ -308,14 +319,14 @@
     def _():
         done(piece, yfs_sem)
 
-    done(buf_a.at[0, pl.ds(0, 2 * L - 1)], as_sem.at[0])
-    done(buf_b.at[0, pl.ds(0, Z * Y // 2 - 1)], bs_sem.at[0])
-    done(buf_a.at[1, pl.ds(0, 2 * L - 1)], as_sem.at[1])
-    done(buf_b.at[1, pl.ds(0, Z * Y // 2 - 1)], bs_sem.at[1])
-    done(buf_a.at[2, pl.ds(0, 2 * L - 1)], as_sem.at[2])
-
-    ray_ref[...] = nt(nn(inverse, unpacked(third(2))[:, :24] / ROWS), inverse)
-    done(buf_b.at[2, pl.ds(0, Z * Y // 2 - 1)], bs_sem.at[2])
+    for step in range(3):
+        done(buf_c.at[0, step, pl.ds(0, 7)], cs_sem.at[0, step])
+    for step in range(3):
+        done(buf_c.at[1, step, pl.ds(0, 7)], cs_sem.at[1, step])
+    done(buf_a.at[pl.ds(0, 2 * L - 1)], as_sem)
+
+    ray_ref[...] = nt(nn(inverse, unpacked(third())[:, :24] / ROWS), inverse)
+    done(buf_b.at[pl.ds(0, Z * Y // 2 - 1)], bs_sem)
 
 
 def body(hamiltonian_blocks, block_rows, block_cols, current_states, previous_steps):
@@ -346,11 +357,13 @@
             pltpu.VMEM((K, OWNED), F32),
             pltpu.VMEM((K, SEG), F32),
             pltpu.VMEM((K, SEG), F32),
-            pltpu.VMEM((3, 2, 8, B), F32),
-            pltpu.VMEM((3, 2 * L, 8, B), F32),
-            pltpu.VMEM((3, Z * Y // 2, 8, B), F32),
+            pltpu.VMEM((2, 8, B), F32),
+            pltpu.VMEM((2, 3, 8, B), F32),
+            pltpu.VMEM((2 * L, 8, B), F32),
+            pltpu.VMEM((Z * Y // 2, 8, B), F32),
+            pltpu.VMEM((2, 3, 8, 8, B), F32),
             dma((5,)), dma, dma, dma, dma, dma, dma, dma, dma, dma, dma, dma, dma,
-            dma, dma, dma, dma, dma((3,)), dma((3,)), dma((3,)), dma((3,)), regular, regular,
+            dma, dma, dma, dma, dma, dma, dma((2, 3)), dma, dma, dma((2, 3)), regular, regular,
         ],
         compiler_params=pltpu.CompilerParams(collective_id=0, has_side_effects=True, vmem_limit_bytes=62 * 1024 * 1024),
         name="lobpcg_step",

time: 62.2 us -> 61.6 us (level)
  no operation moved by 1% of the time
where the time goes in v4:
time: 61.6 us; the launch traced here: 61.4 us
  Pallas kernels  58.8 us (95%)
  local copies, waits for them, and re-layouts  1.96 us (3%)
  between operations  0.65 us (1%)
    pallas_call x1, Pallas kernels, body(): pl.pallas_call(kernel, out_shape=(jax.ShapeDtypeStruct((3 * K, SHARE), F3...  58.8 us
    unnamed x4, local copies, waits for them, and re-layouts  1.96 us

profile of v4, /device:TPU:1, one launch (start us, length us, event | category | flops | bytes accessed | tf_op | source)
XLA Modules:
  0.0 61.4 jit_solution(2755697631930150375)
XLA Ops:
  0.6 58.8 %lobpcg_step.1 = (f32[24,256]{1,0:T(8,128)}, f32[24,24]{1,0:T(8,128)}) custom-call(s32[4]{0:T(128)} %bitcast.4, s32[4]{0:T(128)} %bitcast.5, f32[4,128,128]{2,1,0:T(8,128)} %bitcast.3, f32[8,4096]{1,0:T(8,128)} %x_ref.1, f32[8,4096]{1,0:T(8,128)} %p_ref.1), custom_call_target="tpu_custom_call" | custom-call | tf_op jit(solution)/shard_map/lobpcg_step/pallas_call | solution.py:335
  59.5 0.0 copy-start
  59.5 1.4 %copy.9 = f32[24,256]{1,0:T(8,128)} copy(f32[24,256]{1,0:T(8,128)} %get-tuple-element.4) | data formatting | bytes 49152
  60.8 0.0 copy-done
  60.8 0.6 copy.10
Async XLA Ops:
  59.5 1.4 %copy-start = (f32[24,24]{1,0:T(8,128)S(1)}, f32[24,24]{1,0:T(8,128)}, u32[]{:S(2)}) copy-start(f32[24,24]{1,0:T(8,128)} %get-tuple-element.5) | copy-start | bytes 6916

commit v5 on v4

--- a/solution.py
+++ b/solution.py
@@ -71,8 +71,8 @@
 
 
 def kernel(rows_ref, cols_ref, h_ref, x_ref, p_ref, q_ref, ray_ref,
-           rows, cols, h, x, x_far, p, p_far, p_pick, asked, wanted, m, m_near, d, got, part, other, piece, y, y_far, mine,
-           line, buf_a, buf_b, buf_c, load_sem, x_sem, xs_sem, m_sem, ms_sem, want_sem, wants_sem, p_sem, ps_sem, d_sem, ds_sem, o_sem, os_sem,
+           rows, cols, h, x, p, pick, far, asked, wanted, m, m_near, d, got, part, other, piece, y, y_far, mine,
+           line, buf_a, buf_b, buf_c, load_sem, m_sem, ms_sem, want_sem, wants_sem, f_sem, fs_sem, d_sem, ds_sem, o_sem, os_sem,
            y_sem, ys_sem, yfar_sem, yfs_sem, a_sem, b_sem, c_sem, as_sem, bs_sem, cs_sem, step2, step3):
     r, c = lax.axis_index("row"), lax.axis_index("col")
     z, y_lo, l, y_hi = rem(r, Z), div(r, Z), rem(c, L), div(c, L)
@@ -118,15 +118,24 @@
     for load in loads:
         load.start()
 
+    for load in loads[:2]:
+        load.wait()
+    row_at = [jnp.full((K, B), rows[n], jnp.int32) for n in range(NB)]
+    col_at = [jnp.full((K, B), cols[n], jnp.int32) for n in range(NB)]
+    asks = jnp.zeros((8, B), jnp.int32)
+    for n in range(NB):
+        asks = jnp.where(row_ids((8, B)) == n, col_at[n], asks)
+    asked[...] = asks
+
+    @pl.when(jnp.logical_not(reads))
+    def _():
+        wanted[...] = asks
+
     pl.semaphore_wait(barrier, Z - 1 + Y - 1 + L - 1 + 2 * reads.astype(jnp.int32))
 
     @pl.when(reads)
     def _():
-        send(x_ref, x_far, xs_sem, x_sem, user(l))
-
-    @pl.when(jnp.logical_not(reads))
-    def _():
-        pltpu.make_async_copy(x_ref, x_far, x_sem).start()
+        send(asked, wanted, wants_sem, want_sem, source)
 
     greet(Y, step2, lambda k: at(rem(yy + k, Y), z, l))
 
@@ -137,39 +146,41 @@
             found = [jnp.where(places[n] == b, here, found[n]) for n in range(NB)]
         return found
 
-    for load in loads[:4]:
+    for load in loads[2:]:
         load.wait()
-    row_at = [jnp.full((K, B), rows[n], jnp.int32) for n in range(NB)]
-    col_at = [jnp.full((K, B), cols[n], jnp.int32) for n in range(NB)]
-    x_row = blocks(x, row_at)
-    m_x = jnp.concatenate([nn(x_row[n], h[n]) for n in range(NB)], 1)
-
-    asks = jnp.zeros((8, B), jnp.int32)
-    for n in range(NB):
-        asks = jnp.where(row_ids((8, B)) == n, col_at[n], asks)
+    x_row, p_row = blocks(x, row_at), blocks(p, row_at)
+    both = [nn(jnp.concatenate([x_row[n], p_row[n]], 0), h[n]) for n in range(NB)]
+    m_x, m_p = (jnp.concatenate([both[n][k : k + K] for n in range(NB)], 1) for k in (0, K))
 
     @pl.when(reads)
     def _():
         m[...] = m_x
-        asked[...] = asks
         send(m, m_near, ms_sem, m_sem, source)
-        send(asked, wanted, wants_sem, want_sem, source)
 
     @pl.when(jnp.logical_not(reads))
     def _():
         m_near[...] = m_x
-        wanted[...] = asks
 
     pl.semaphore_wait(step2, Y - 1)
     greet(Z, step3, lambda k: at(yy, rem(z + k, Z), l))
-    loads[4].wait()
-    p_row = blocks(p, row_at)
-    m_p = jnp.concatenate([nn(p_row[n], h[n]) for n in range(NB)], 1)
-
-    done(x_far, x_sem)
-    x_col = blocks(x_far, col_at)
-    direct = [nt(x_col[n], h[n]) for n in range(NB)]
-    xc = jnp.concatenate(x_col, 1)
+
+    @pl.when(reads)
+    def _():
+        done(wanted, want_sem)
+
+    want = wanted[...]
+    want_at = [jnp.broadcast_to(want[n : n + 1], (K, B)) for n in range(NB)]
+    picked = jnp.concatenate([jnp.concatenate(blocks(x, want_at), 1), jnp.concatenate(blocks(p, want_at), 1)], 0)
+
+    @pl.when(reads)
+    def _():
+        pick[...] = picked
+        send(pick, far, fs_sem, f_sem, user(l))
+
+    @pl.when(jnp.logical_not(reads))
+    def _():
+        far[...] = picked
+
     near_last = (4, 5, 3, 6, 2, 7, 1, 0)
 
     y_par, y_pair = rem(yy, 2), div(yy, 2)
@@ -209,23 +220,24 @@
         done(buf_c.at[i, step], c_sem.at[i, step])
         return summed([buf_c[i, step, s] for s in range(8)])
 
-    pl.semaphore_wait(step3, Z - 1)
-    start(0, 0, nt(m_x, padded(xc)) + nt(xc, padded(m_x)))
-
+    @pl.when(reads)
+    def _():
+        done(far, f_sem)
+
+    xc, p_col = far[:K], far[K:]
+    direct = [nt(xc[:, n * B : (n + 1) * B], h[n]) for n in range(NB)]
 
     @pl.when(reads)
     def _():
         done(m_near, m_sem)
-        done(wanted, want_sem)
-
-    want = wanted[...]
-    want_at = [jnp.broadcast_to(want[n : n + 1], (K, B)) for n in range(NB)]
+
     terms = [direct[n] for n in range(NB)] + [m_near[:, n * B : (n + 1) * B] for n in range(NB)]
     for b in range(SEGB):
         total = jnp.zeros((K, B), F32)
         for place, term in zip(row_at + want_at, terms):
             total = total + jnp.where(place == b, term, 0.0)
         d[:, b * B : (b + 1) * B] = total
+    pl.semaphore_wait(step3, Z - 1)
 
     def share(l_at):
         return pl.ds(pl.multiple_of(l_at * OWNED, OWNED), OWNED)
@@ -235,15 +247,7 @@
         send(d.at[:, share(j)], got.at[l], ds_sem, d_sem, at(yy, z, j))
     pltpu.make_async_copy(d.at[:, share(l)], got.at[l], d_sem).start()
 
-    @pl.when(reads)
-    def _():
-        p_pick[...] = jnp.concatenate(blocks(p, want_at), 1)
-        send(p_pick, p_far, ps_sem, p_sem, user(l))
-
-    @pl.when(jnp.logical_not(reads))
-    def _():
-        p_far[...] = jnp.concatenate(blocks(p, col_at), 1)
-
+    start(0, 0, nt(m_x, padded(xc)) + nt(xc, padded(m_x)))
     start(0, 1, finish(0, 0))
     done(got, d_sem)
     part[...] = summed([got[s] for s in range(L)])
@@ -278,11 +282,6 @@
     start(1, 0, packed(nt(basis, padded(basis))))
     taken = nn(theta, jnp.concatenate([m_x, xc, x[:, own]], 1))
 
-    @pl.when(reads)
-    def _():
-        done(p_far, p_sem)
-
-    p_col = p_far[...]
     done(y, y_sem)
     y_row = blocks(y, row_at)
     m_r = jnp.concatenate([nn(y_row[n], h[n]) for n in range(NB)], 1) - taken[:, : NB * B]
@@ -299,16 +298,12 @@
 
     @pl.when(reads)
     def _():
-        done(x_ref, xs_sem)
-
-    @pl.when(reads)
-    def _():
         done(m, ms_sem)
         done(asked, wants_sem)
 
     @pl.when(reads)
     def _():
-        done(p_pick, ps_sem)
+        done(pick, fs_sem)
 
     done(got.at[pl.ds(0, L - 1)], ds_sem)
     done(part, os_sem)
@@ -343,9 +338,8 @@
             pltpu.VMEM((NB, B, B), F32),
             pltpu.VMEM((K, SEG), F32),
             pltpu.VMEM((K, SEG), F32),
-            pltpu.VMEM((K, SEG), F32),
-            pltpu.VMEM((K, NB * B), F32),
-            pltpu.VMEM((K, NB * B), F32),
+            pltpu.VMEM((2 * K, NB * B), F32),
+            pltpu.VMEM((2 * K, NB * B), F32),
             pltpu.VMEM((8, B), jnp.int32),
             pltpu.VMEM((8, B), jnp.int32),
             pltpu.VMEM((K, NB * B), F32),
@@ -362,7 +356,7 @@
             pltpu.VMEM((2 * L, 8, B), F32),
             pltpu.VMEM((Z * Y // 2, 8, B), F32),
             pltpu.VMEM((2, 3, 8, 8, B), F32),
-            dma((5,)), dma, dma, dma, dma, dma, dma, dma, dma, dma, dma, dma, dma,
+            dma((5,)), dma, dma, dma, dma, dma, dma, dma, dma, dma, dma,
             dma, dma, dma, dma, dma, dma, dma((2, 3)), dma, dma, dma((2, 3)), regular, regular,
         ],
         compiler_params=pltpu.CompilerParams(collective_id=0, has_side_effects=True, vmem_limit_bytes=62 * 1024 * 1024),

time: 61.6 us -> 61.6 us (level); the launches traced: 61.4 us -> 60.5 us
  Pallas kernels: 58.8 us -> 57.9 us
    pallas_call x1, Pallas kernels: 58.8 us -> 57.9 us  [body(): pl.pallas_call(kernel, out_shape=(jax.ShapeDtypeStruct((3 * K, SHARE), F3...]
where the time goes in v5:
time: 61.6 us; the launch traced here: 60.5 us
  Pallas kernels  57.9 us (94%)
  local copies, waits for them, and re-layouts  1.96 us (3%)
  between operations  0.65 us (1%)
    pallas_call x1, Pallas kernels, body(): pl.pallas_call(kernel, out_shape=(jax.ShapeDtypeStruct((3 * K, SHARE), F3...  57.9 us
    unnamed x4, local copies, waits for them, and re-layouts  1.96 us

profile of v5, /device:TPU:1, one launch (start us, length us, event | category | flops | bytes accessed | tf_op | source)
XLA Modules:
  0.0 60.5 jit_solution(8604973622652963163)
XLA Ops:
  0.6 57.9 %lobpcg_step.1 = (f32[24,256]{1,0:T(8,128)}, f32[24,24]{1,0:T(8,128)}) custom-call(s32[4]{0:T(128)} %bitcast.4, s32[4]{0:T(128)} %bitcast.5, f32[4,128,128]{2,1,0:T(8,128)} %bitcast.3, f32[8,4096]{1,0:T(8,128)} %x_ref.1, f32[8,4096]{1,0:T(8,128)} %p_ref.1), custom_call_target="tpu_custom_call" | custom-call | tf_op jit(solution)/shard_map/lobpcg_step/pallas_call | solution.py:330
  58.5 0.0 copy-start
  58.6 1.4 %copy.9 = f32[24,256]{1,0:T(8,128)} copy(f32[24,256]{1,0:T(8,128)} %get-tuple-element.4) | data formatting | bytes 49152
  59.9 0.0 copy-done
  59.9 0.6 copy.10
Async XLA Ops:
  58.5 1.4 %copy-start = (f32[24,24]{1,0:T(8,128)S(1)}, f32[24,24]{1,0:T(8,128)}, u32[]{:S(2)}) copy-start(f32[24,24]{1,0:T(8,128)} %get-tuple-element.5) | copy-start | bytes 6916

commit v6 on v5

--- a/solution.py
+++ b/solution.py
@@ -47,13 +47,34 @@
     return terms[0]
 
 
+def folded(t):
+    return t[0:4] + pltpu.roll(t[4:8], 64, 1)
+
+
+def unfolded(t):
+    t = jnp.concatenate([t, pltpu.roll(t, 64, 1)], 0)
+    return jnp.where(lane_ids(t.shape) < 64, t, 0.0)
+
+
+def between(a, low, high):
+    lanes = lane_ids(a.shape)
+    return jnp.where(jnp.logical_and(lanes >= low, lanes < high), a, 0.0)
+
+
 def packed(a):
-    return a[0:8] + pltpu.roll(a[8:16], 32, 1) + pltpu.roll(a[16:24], 64, 1)
+    return folded(between(a[0:8], 0, 24) + pltpu.roll(between(a[8:16], 8, 24), 16, 1) + pltpu.roll(between(a[16:24], 16, 24), 24, 1))
 
 
 def unpacked(t):
-    a = jnp.concatenate([t, pltpu.roll(t, 96, 1), pltpu.roll(t, 64, 1)], 0)
-    return jnp.where(lane_ids(a.shape) < 24, a, 0.0)
+    t = unfolded(t)
+    a = jnp.concatenate([between(t, 0, 24), between(pltpu.roll(t, 112, 1), 8, 24), between(pltpu.roll(t, 104, 1), 16, 24)], 0)
+    same = lax.shift_right_logical(lane_ids(a.shape), 3) == lax.shift_right_logical(row_ids(a.shape), 3)
+    return jnp.where(same, 0.5 * a, a)
+
+
+def symmetric(a):
+    unit = (lane_ids((24, B)) == row_ids((24, B))).astype(F32)
+    return a + nt(unit, padded(a))
 
 
 def inverse_factor(gram):
@@ -247,7 +268,7 @@
         send(d.at[:, share(j)], got.at[l], ds_sem, d_sem, at(yy, z, j))
     pltpu.make_async_copy(d.at[:, share(l)], got.at[l], d_sem).start()
 
-    start(0, 0, nt(m_x, padded(xc)) + nt(xc, padded(m_x)))
+    start(0, 0, folded(nt(m_x, padded(xc)) + nt(xc, padded(m_x))))
     start(0, 1, finish(0, 0))
     done(got, d_sem)
     part[...] = summed([got[s] for s in range(L)])
@@ -273,7 +294,7 @@
         send(piece, y.at[:, mine_of], ys_sem, y_sem, at(yy, z, rem(l + k, L)))
     pltpu.make_async_copy(piece, y.at[:, mine_of], y_sem).start()
 
-    theta = finish(0, 2)[:, :K] / ROWS
+    theta = unfolded(finish(0, 2))[:, :K] / ROWS
     half = pl.ds(pl.multiple_of(l * OWNED + y_hi * SHARE, SHARE), SHARE)
     half_of = pl.ds(pl.multiple_of(y_hi * SHARE, SHARE), SHARE)
     own = pl.ds(pl.multiple_of(c * SHARE, SHARE), SHARE)
@@ -293,7 +314,7 @@
     start(1, 1, finish(1, 0))
     second()
     start(1, 2, finish(1, 1))
-    inverse = inverse_factor(unpacked(finish(1, 2)) / ROWS)[:, :24]
+    inverse = inverse_factor(symmetric(unpacked(finish(1, 2))) / ROWS)[:, :24]
     q_ref[...] = nn(inverse, jnp.concatenate([y[:, own] - taken[:, 2 * NB * B :], x[:, own], p[:, own]], 0))
 
     @pl.when(reads)
@@ -320,7 +341,8 @@
         done(buf_c.at[1, step, pl.ds(0, 7)], cs_sem.at[1, step])
     done(buf_a.at[pl.ds(0, 2 * L - 1)], as_sem)
 
-    ray_ref[...] = nt(nn(inverse, unpacked(third())[:, :24] / ROWS), inverse)
+    half_way = nn(inverse, unpacked(third())[:, :24] / ROWS)
+    ray_ref[...] = nt(half_way, inverse) + nt(inverse, half_way)
     done(buf_b.at[pl.ds(0, Z * Y // 2 - 1)], bs_sem)
 
 
@@ -351,11 +373,11 @@
             pltpu.VMEM((K, OWNED), F32),
             pltpu.VMEM((K, SEG), F32),
             pltpu.VMEM((K, SEG), F32),
-            pltpu.VMEM((2, 8, B), F32),
-            pltpu.VMEM((2, 3, 8, B), F32),
-            pltpu.VMEM((2 * L, 8, B), F32),
-            pltpu.VMEM((Z * Y // 2, 8, B), F32),
-            pltpu.VMEM((2, 3, 8, 8, B), F32),
+            pltpu.VMEM((2, 4, B), F32),
+            pltpu.VMEM((2, 3, 4, B), F32),
+            pltpu.VMEM((2 * L, 4, B), F32),
+            pltpu.VMEM((Z * Y // 2, 4, B), F32),
+            pltpu.VMEM((2, 3, 8, 4, B), F32),
             dma((5,)), dma, dma, dma, dma, dma, dma, dma, dma, dma, dma,
             dma, dma, dma, dma, dma, dma, dma((2, 3)), dma, dma, dma((2, 3)), regular, regular,
         ],

time: 61.6 us -> 60.6 us (0.984); the launches traced: 60.5 us -> 60.3 us
  no operation moved by 1% of the time
where the time goes in v6:
time: 60.6 us; the launch traced here: 60.3 us
  Pallas kernels  57.7 us (95%)
  local copies, waits for them, and re-layouts  1.96 us (3%)
  between operations  0.65 us (1%)
    pallas_call x1, Pallas kernels, body(): pl.pallas_call(kernel, out_shape=(jax.ShapeDtypeStruct((3 * K, SHARE), F3...  57.7 us
    unnamed x4, local copies, waits for them, and re-layouts  1.96 us

profile of v6, /device:TPU:1, one launch (start us, length us, event | category | flops | bytes accessed | tf_op | source)
XLA Modules:
  0.0 60.3 jit_solution(11492487926955708952)
XLA Ops:
  0.6 57.7 %lobpcg_step.1 = (f32[24,256]{1,0:T(8,128)}, f32[24,24]{1,0:T(8,128)}) custom-call(s32[4]{0:T(128)} %bitcast.4, s32[4]{0:T(128)} %bitcast.5, f32[4,128,128]{2,1,0:T(8,128)} %bitcast.3, f32[8,4096]{1,0:T(8,128)} %x_ref.1, f32[8,4096]{1,0:T(8,128)} %p_ref.1), custom_call_target="tpu_custom_call" | custom-call | tf_op jit(solution)/shard_map/lobpcg_step/pallas_call | solution.py:352
  58.3 0.0 copy-start
  58.3 1.4 %copy.9 = f32[24,256]{1,0:T(8,128)} copy(f32[24,256]{1,0:T(8,128)} %get-tuple-element.4) | data formatting | bytes 49152
  59.7 0.0 copy-done
  59.7 0.6 copy.10
Async XLA Ops:
  58.3 1.4 %copy-start = (f32[24,24]{1,0:T(8,128)S(1)}, f32[24,24]{1,0:T(8,128)}, u32[]{:S(2)}) copy-start(f32[24,24]{1,0:T(8,128)} %get-tuple-element.5) | copy-start | bytes 6916

commit v7 on v6

--- a/solution.py
+++ b/solution.py
@@ -109,6 +109,11 @@
     def done(ref, sem):
         pltpu.make_async_copy(ref, ref, sem).wait()
 
+    loads = [pltpu.make_async_copy(src, dst, load_sem.at[i]) for i, (src, dst) in enumerate(
+        ((rows_ref, rows), (cols_ref, cols), (x_ref, x), (h_ref, h), (p_ref, p)))]
+    for load in loads[:2]:
+        load.start()
+
     reads = c != 0
     q = rem(r + c, N_ROW)
     turned = jnp.logical_and(div(q, Z) == 0, z + l >= Z).astype(jnp.int32)
@@ -126,6 +131,9 @@
         pl.semaphore_signal(barrier, inc=1, device_id=source, device_id_type=MESH)
         pl.semaphore_signal(barrier, inc=1, device_id=user(l), device_id_type=MESH)
 
+    for load in loads[2:]:
+        load.start()
+
     def greet(n, sem, place):
         for k in range(1, n):
             pl.semaphore_signal(sem, inc=1, device_id=place(k), device_id_type=MESH)
@@ -133,11 +141,6 @@
     greet(Z, barrier, lambda k: at(yy, rem(z + k, Z), l))
     greet(Y, barrier, lambda k: at(rem(yy + k, Y), z, l))
     greet(L, barrier, lambda k: at(yy, z, rem(l + k, L)))
-
-    loads = [pltpu.make_async_copy(src, dst, load_sem.at[i]) for i, (src, dst) in enumerate(
-        ((rows_ref, rows), (cols_ref, cols), (x_ref, x), (h_ref, h), (p_ref, p)))]
-    for load in loads:
-        load.start()
 
     for load in loads[:2]:
         load.wait()
@@ -182,25 +185,26 @@
     def _():
         m_near[...] = m_x
 
+    @pl.when(reads)
+    def _():
+        done(wanted, want_sem)
+
+    want = wanted[...]
+    want_at = [jnp.broadcast_to(want[n : n + 1], (K, B)) for n in range(NB)]
+    for i, held in enumerate((x, p)):
+        picked = jnp.concatenate(blocks(held, want_at), 1)
+
+        @pl.when(reads)
+        def _(i=i, picked=picked):
+            pick[i] = picked
+            send(pick.at[i], far.at[i], fs_sem.at[i], f_sem.at[i], user(l))
+
+        @pl.when(jnp.logical_not(reads))
+        def _(i=i, picked=picked):
+            far[i] = picked
+
     pl.semaphore_wait(step2, Y - 1)
     greet(Z, step3, lambda k: at(yy, rem(z + k, Z), l))
-
-    @pl.when(reads)
-    def _():
-        done(wanted, want_sem)
-
-    want = wanted[...]
-    want_at = [jnp.broadcast_to(want[n : n + 1], (K, B)) for n in range(NB)]
-    picked = jnp.concatenate([jnp.concatenate(blocks(x, want_at), 1), jnp.concatenate(blocks(p, want_at), 1)], 0)
-
-    @pl.when(reads)
-    def _():
-        pick[...] = picked
-        send(pick, far, fs_sem, f_sem, user(l))
-
-    @pl.when(jnp.logical_not(reads))
-    def _():
-        far[...] = picked
 
     near_last = (4, 5, 3, 6, 2, 7, 1, 0)
 
@@ -243,9 +247,9 @@
 
     @pl.when(reads)
     def _():
-        done(far, f_sem)
-
-    xc, p_col = far[:K], far[K:]
+        done(far.at[0], f_sem.at[0])
+
+    xc = far[0]
     direct = [nt(xc[:, n * B : (n + 1) * B], h[n]) for n in range(NB)]
 
     @pl.when(reads)
@@ -303,6 +307,11 @@
     start(1, 0, packed(nt(basis, padded(basis))))
     taken = nn(theta, jnp.concatenate([m_x, xc, x[:, own]], 1))
 
+    @pl.when(reads)
+    def _():
+        done(far.at[1], f_sem.at[1])
+
+    p_col = far[1]
     done(y, y_sem)
     y_row = blocks(y, row_at)
     m_r = jnp.concatenate([nn(y_row[n], h[n]) for n in range(NB)], 1) - taken[:, : NB * B]
@@ -324,7 +333,8 @@
 
     @pl.when(reads)
     def _():
-        done(pick, fs_sem)
+        for i in range(2):
+            done(pick.at[i], fs_sem.at[i])
 
     done(got.at[pl.ds(0, L - 1)], ds_sem)
     done(part, os_sem)
@@ -360,8 +370,8 @@
             pltpu.VMEM((NB, B, B), F32),
             pltpu.VMEM((K, SEG), F32),
             pltpu.VMEM((K, SEG), F32),
-            pltpu.VMEM((2 * K, NB * B), F32),
-            pltpu.VMEM((2 * K, NB * B), F32),
+            pltpu.VMEM((2, K, NB * B), F32),
+            pltpu.VMEM((2, K, NB * B), F32),
             pltpu.VMEM((8, B), jnp.int32),
             pltpu.VMEM((8, B), jnp.int32),
             pltpu.VMEM((K, NB * B), F32),
@@ -378,7 +388,7 @@
             pltpu.VMEM((2 * L, 4, B), F32),
             pltpu.VMEM((Z * Y // 2, 4, B), F32),
             pltpu.VMEM((2, 3, 8, 4, B), F32),
-            dma((5,)), dma, dma, dma, dma, dma, dma, dma, dma, dma, dma,
+            dma((5,)), dma, dma, dma, dma, dma((2,)), dma((2,)), dma, dma, dma, dma,
             dma, dma, dma, dma, dma, dma, dma((2, 3)), dma, dma, dma((2, 3)), regular, regular,
         ],
         compiler_params=pltpu.CompilerParams(collective_id=0, has_side_effects=True, vmem_limit_bytes=62 * 1024 * 1024),

time: 60.6 us -> 60.3 us (level)
  Pallas kernels: 57.7 us -> 57 us
    pallas_call x1, Pallas kernels: 57.7 us -> 57 us  [body(): pl.pallas_call(kernel, out_shape=(jax.ShapeDtypeStruct((3 * K, SHARE), F3...]
where the time goes in v7:
time: 60.3 us; the launch traced here: 59.6 us
  Pallas kernels  57 us (95%)
  local copies, waits for them, and re-layouts  1.96 us (3%)
  between operations  0.65 us (1%)
    pallas_call x1, Pallas kernels, body(): pl.pallas_call(kernel, out_shape=(jax.ShapeDtypeStruct((3 * K, SHARE), F3...  57 us
    unnamed x4, local copies, waits for them, and re-layouts  1.96 us

profile of v7, /device:TPU:1, one launch (start us, length us, event | category | flops | bytes accessed | tf_op | source)
XLA Modules:
  0.0 59.6 jit_solution(15778314298385040331)
XLA Ops:
  0.6 57.0 %lobpcg_step.1 = (f32[24,256]{1,0:T(8,128)}, f32[24,24]{1,0:T(8,128)}) custom-call(s32[4]{0:T(128)} %bitcast.4, s32[4]{0:T(128)} %bitcast.5, f32[4,128,128]{2,1,0:T(8,128)} %bitcast.3, f32[8,4096]{1,0:T(8,128)} %x_ref.1, f32[8,4096]{1,0:T(8,128)} %p_ref.1), custom_call_target="tpu_custom_call" | custom-call | tf_op jit(solution)/shard_map/lobpcg_step/pallas_call | solution.py:362
  57.6 0.0 copy-start
  57.6 1.4 %copy.9 = f32[24,256]{1,0:T(8,128)} copy(f32[24,256]{1,0:T(8,128)} %get-tuple-element.4) | data formatting | bytes 49152
  59.0 0.0 copy-done
  59.0 0.6 %copy.10 = f32[24,24]{1,0:T(8,128)} copy(f32[24,24]{1,0:T(8,128)S(1)} %copy-done) | data formatting | bytes 4608
Async XLA Ops:
  57.6 1.4 %copy-start = (f32[24,24]{1,0:T(8,128)S(1)}, f32[24,24]{1,0:T(8,128)}, u32[]{:S(2)}) copy-start(f32[24,24]{1,0:T(8,128)} %get-tuple-element.5) | copy-start | bytes 6916

commit v8 on v7

--- a/solution.py
+++ b/solution.py
@@ -16,7 +16,8 @@
 N_ROW, N_COL = Z * YL, L * YH
 K, B, SEGB, NB = 8, 128, 32, 4
 SEG = SEGB * B
-SHARE, OWNED = SEG // N_COL, SEG // L
+X = L // 2
+SHARE, OWNED = SEG // N_COL, SEG // X
 ROWS = N_ROW * SEG
 rem, div = lax.rem, lax.div
 
@@ -92,12 +93,15 @@
 
 
 def kernel(rows_ref, cols_ref, h_ref, x_ref, p_ref, q_ref, ray_ref,
-           rows, cols, h, x, p, pick, far, asked, wanted, m, m_near, d, got, part, other, piece, y, y_far, mine,
+           rows, cols, h, x, p, pick, far, asked, wanted, m, m_near, d, got, part, other, piece, products, y, y_far, mine,
            line, buf_a, buf_b, buf_c, load_sem, m_sem, ms_sem, want_sem, wants_sem, f_sem, fs_sem, d_sem, ds_sem, o_sem, os_sem,
            y_sem, ys_sem, yfar_sem, yfs_sem, a_sem, b_sem, c_sem, as_sem, bs_sem, cs_sem, step2, step3):
     r, c = lax.axis_index("row"), lax.axis_index("col")
     z, y_lo, l, y_hi = rem(r, Z), div(r, Z), rem(c, L), div(c, L)
     yy = y_hi * YL + y_lo
+    xx = div(l, 2)
+    main = rem(l, 2) == 1
+    aside = jnp.logical_not(main)
 
     def at(y_at, z_at, l_at):
         return (rem(y_at, YL) * Z + z_at, div(y_at, YL) * L + l_at)
@@ -214,20 +218,32 @@
 
     def first(tile):
         mine[0] = tile
-        for k in range(2 * L - 1):
-            y_to = 2 * y_pair + rem(y_par + 1 + k // L, 2)
-            send(mine.at[0], buf_a.at[slot_a], as_sem, a_sem, at(y_to, z, rem(l + near_last[k % L], L)))
-        pltpu.make_async_copy(mine.at[0], buf_a.at[slot_a], a_sem).start()
+        for y_k in (1, 0):
+            for x_k in (2, 1, 3, 0):
+                to = at(2 * y_pair + rem(y_par + y_k, 2), z, 2 * rem(xx + x_k, X) + 1)
+                if y_k or x_k:
+                    send(mine.at[0], buf_a.at[slot_a], as_sem, a_sem, to)
+                else:
+                    @pl.when(main)
+                    def _():
+                        pltpu.make_async_copy(mine.at[0], buf_a.at[slot_a], a_sem).start()
+
+                    @pl.when(aside)
+                    def _(to=to):
+                        send(mine.at[0], buf_a.at[slot_a], as_sem, a_sem, to)
 
     def second():
-        done(buf_a, a_sem)
-        mine[1] = summed([buf_a[s] for s in range(2 * L)])
-        for y_k in (2, 1, 3, 0):
-            for z_k in near_last:
-                if y_k or z_k:
-                    y_to = 2 * rem(y_pair + y_k, Y // 2) + y_par
-                    send(mine.at[1], buf_b.at[slot_b], bs_sem, b_sem, at(y_to, rem(z + z_k, Z), l))
-        pltpu.make_async_copy(mine.at[1], buf_b.at[slot_b], b_sem).start()
+        @pl.when(main)
+        def _():
+            done(buf_a, a_sem)
+            mine[1] = summed([buf_a[s] for s in range(2 * L)])
+            for y_k in (2, 1, 3, 0):
+                for z_k in near_last:
+                    for core in (0, 1):
+                        if y_k or z_k or core == 0:
+                            to = at(2 * rem(y_pair + y_k, Y // 2) + y_par, rem(z + z_k, Z), 2 * xx + core)
+                            send(mine.at[1], buf_b.at[slot_b], bs_sem, b_sem, to)
+            pltpu.make_async_copy(mine.at[1], buf_b.at[slot_b], b_sem).start()
 
     def third():
         done(buf_b, b_sem)
@@ -264,47 +280,61 @@
         d[:, b * B : (b + 1) * B] = total
     pl.semaphore_wait(step3, Z - 1)
 
-    def share(l_at):
-        return pl.ds(pl.multiple_of(l_at * OWNED, OWNED), OWNED)
-
-    for k in near_last[:-1]:
-        j = rem(l + k, L)
-        send(d.at[:, share(j)], got.at[l], ds_sem, d_sem, at(yy, z, j))
-    pltpu.make_async_copy(d.at[:, share(l)], got.at[l], d_sem).start()
+    def share(x_at):
+        return pl.ds(pl.multiple_of(x_at * OWNED, OWNED), OWNED)
+
+    for k in (2, 1, 3, 0):
+        j = rem(xx + k, X)
+        src, to = d.at[:, share(j)], at(yy, z, 2 * j + 1)
+        if k:
+            send(src, got.at[l], ds_sem, d_sem, to)
+        else:
+            @pl.when(main)
+            def _(src=src):
+                pltpu.make_async_copy(src, got.at[l], d_sem).start()
+
+            @pl.when(aside)
+            def _(src=src, to=to):
+                send(src, got.at[l], ds_sem, d_sem, to)
 
     start(0, 0, folded(nt(m_x, padded(xc)) + nt(xc, padded(m_x))))
     start(0, 1, finish(0, 0))
-    done(got, d_sem)
-    part[...] = summed([got[s] for s in range(L)])
-    send(part, other, os_sem, o_sem, (r, rem(y_hi + 1, YH) * L + l))
+    @pl.when(main)
+    def _():
+        done(got, d_sem)
+        part[...] = summed([got[s] for s in range(L)])
+        send(part, other, os_sem, o_sem, (r, rem(y_hi + 1, YH) * L + l))
+
     start(0, 2, finish(0, 1))
-    done(other, o_sem)
-    piece[...] = part[...] + other[...]
-
-    mine_of = share(l)
-    for l_to in near_last:
-        if l_to:
+
+    @pl.when(main)
+    def _():
+        done(other, o_sem)
+        piece[...] = part[...] + other[...]
+        mine_of = share(xx)
+        for l_to in near_last:
             send(piece, y_far.at[:, mine_of], yfs_sem, yfar_sem, user(l_to))
-        else:
-            @pl.when(c == 0)
-            def _():
-                pltpu.make_async_copy(piece, y_far.at[:, mine_of], yfar_sem).start()
-
-            @pl.when(reads)
-            def _():
-                send(piece, y_far.at[:, mine_of], yfs_sem, yfar_sem, user(0))
-
-    for k in near_last[:-1]:
-        send(piece, y.at[:, mine_of], ys_sem, y_sem, at(yy, z, rem(l + k, L)))
-    pltpu.make_async_copy(piece, y.at[:, mine_of], y_sem).start()
+        for k in near_last[:-1]:
+            send(piece, y.at[:, mine_of], ys_sem, y_sem, at(yy, z, rem(l + k, L)))
+        pltpu.make_async_copy(piece, y.at[:, mine_of], y_sem).start()
 
     theta = unfolded(finish(0, 2))[:, :K] / ROWS
-    half = pl.ds(pl.multiple_of(l * OWNED + y_hi * SHARE, SHARE), SHARE)
-    half_of = pl.ds(pl.multiple_of(y_hi * SHARE, SHARE), SHARE)
     own = pl.ds(pl.multiple_of(c * SHARE, SHARE), SHARE)
-    residual = piece[:, half_of] - nn(theta, x[:, half])
-    basis = jnp.concatenate([residual, x[:, half], p[:, half]], 0)
-    start(1, 0, packed(nt(basis, padded(basis))))
+
+    @pl.when(main)
+    def _():
+        width = OWNED // YH
+        half = pl.ds(pl.multiple_of(xx * OWNED + y_hi * width, width), width)
+        half_of = pl.ds(pl.multiple_of(y_hi * width, width), width)
+        residual = piece[:, half_of] - nn(theta, x[:, half])
+        basis = jnp.concatenate([residual, x[:, half], p[:, half]], 0)
+        products[...] = packed(nt(basis, padded(basis)))
+
+    @pl.when(aside)
+    def _():
+        products[...] = jnp.zeros_like(products)
+
+    start(1, 0, products[...])
     taken = nn(theta, jnp.concatenate([m_x, xc, x[:, own]], 1))
 
     @pl.when(reads)
@@ -336,24 +366,32 @@
         for i in range(2):
             done(pick.at[i], fs_sem.at[i])
 
-    done(got.at[pl.ds(0, L - 1)], ds_sem)
-    done(part, os_sem)
-    done(got.at[pl.ds(0, L - 1)], yfs_sem)
-    done(got.at[pl.ds(0, L - 1)], ys_sem)
-
-    @pl.when(reads)
-    def _():
-        done(piece, yfs_sem)
+    done(got.at[pl.ds(0, X - 1)], ds_sem)
+    done(buf_a.at[pl.ds(0, L - 1)], as_sem)
+
+    @pl.when(aside)
+    def _():
+        done(got.at[0], ds_sem)
+        done(buf_a.at[0], as_sem)
+
+    @pl.when(main)
+    def _():
+        done(part, os_sem)
+        done(got, yfs_sem)
+        done(got.at[pl.ds(0, L - 1)], ys_sem)
 
     for step in range(3):
         done(buf_c.at[0, step, pl.ds(0, 7)], cs_sem.at[0, step])
     for step in range(3):
         done(buf_c.at[1, step, pl.ds(0, 7)], cs_sem.at[1, step])
-    done(buf_a.at[pl.ds(0, 2 * L - 1)], as_sem)
 
     half_way = nn(inverse, unpacked(third())[:, :24] / ROWS)
     ray_ref[...] = nt(half_way, inverse) + nt(inverse, half_way)
-    done(buf_b.at[pl.ds(0, Z * Y // 2 - 1)], bs_sem)
+
+    @pl.when(main)
+    def _():
+        done(buf_b, bs_sem)
+        done(buf_b.at[pl.ds(0, Z * Y // 2 - 1)], bs_sem)
 
 
 def body(hamiltonian_blocks, block_rows, block_cols, current_states, previous_steps):
@@ -381,6 +419,7 @@
             pltpu.VMEM((K, OWNED), F32),
             pltpu.VMEM((K, OWNED), F32),
             pltpu.VMEM((K, OWNED), F32),
+            pltpu.VMEM((4, B), F32),
             pltpu.VMEM((K, SEG), F32),
             pltpu.VMEM((K, SEG), F32),
             pltpu.VMEM((2, 4, B), F32),

time: 60.3 us -> 60.2 us (level)
  no operation moved by 1% of the time
where the time goes in v8:
time: 60.2 us; the launch traced here: 60 us
  Pallas kernels  57.4 us (95%)
  local copies, waits for them, and re-layouts  1.96 us (3%)
  between operations  0.65 us (1%)
    pallas_call x1, Pallas kernels, body(): pl.pallas_call(kernel, out_shape=(jax.ShapeDtypeStruct((3 * K, SHARE), F3...  57.4 us
    unnamed x4, local copies, waits for them, and re-layouts  1.96 us

profile of v8, /device:TPU:1, one launch (start us, length us, event | category | flops | bytes accessed | tf_op | source)
XLA Modules:
  0.0 60.0 jit_solution(12049015376429946786)
XLA Ops:
  0.6 57.4 %lobpcg_step.1 = (f32[24,256]{1,0:T(8,128)}, f32[24,24]{1,0:T(8,128)}) custom-call(s32[4]{0:T(128)} %bitcast.4, s32[4]{0:T(128)} %bitcast.5, f32[4,128,128]{2,1,0:T(8,128)} %bitcast.3, f32[8,4096]{1,0:T(8,128)} %x_ref.1, f32[8,4096]{1,0:T(8,128)} %p_ref.1), custom_call_target="tpu_custom_call" | custom-call | tf_op jit(solution)/shard_map/lobpcg_step/pallas_call | solution.py:400
  58.0 0.0 copy-start
  58.0 1.4 %copy.9 = f32[24,256]{1,0:T(8,128)} copy(f32[24,256]{1,0:T(8,128)} %get-tuple-element.4) | data formatting | bytes 49152
  59.4 0.0 copy-done
  59.4 0.6 copy.10
Async XLA Ops:
  58.0 1.4 %copy-start = (f32[24,24]{1,0:T(8,128)S(1)}, f32[24,24]{1,0:T(8,128)}, u32[]{:S(2)}) copy-start(f32[24,24]{1,0:T(8,128)} %get-tuple-element.5) | copy-start | bytes 6916

commit v9 on v8

--- a/solution.py
+++ b/solution.py
@@ -94,8 +94,8 @@
 
 def kernel(rows_ref, cols_ref, h_ref, x_ref, p_ref, q_ref, ray_ref,
            rows, cols, h, x, p, pick, far, asked, wanted, m, m_near, d, got, part, other, piece, products, y, y_far, mine,
-           line, buf_a, buf_b, buf_c, load_sem, m_sem, ms_sem, want_sem, wants_sem, f_sem, fs_sem, d_sem, ds_sem, o_sem, os_sem,
-           y_sem, ys_sem, yfar_sem, yfs_sem, a_sem, b_sem, c_sem, as_sem, bs_sem, cs_sem, step2, step3):
+           buf_a, buf_b, whole, load_sem, m_sem, ms_sem, want_sem, wants_sem, f_sem, fs_sem, d_sem, ds_sem, o_sem, os_sem,
+           y_sem, ys_sem, yfar_sem, yfs_sem, a_sem, b_sem, w_sem, as_sem, bs_sem, ws_sem, step2, step3):
     r, c = lax.axis_index("row"), lax.axis_index("col")
     z, y_lo, l, y_hi = rem(r, Z), div(r, Z), rem(c, L), div(c, L)
     yy = y_hi * YL + y_lo
@@ -216,50 +216,53 @@
     slot_a = y_par * L + l
     slot_b = y_pair * Z + z
 
-    def first(tile):
-        mine[0] = tile
+    def first(i, tile):
+        mine[i, 0] = tile
+        src, dst = mine.at[i, 0], buf_a.at[i, slot_a]
         for y_k in (1, 0):
             for x_k in (2, 1, 3, 0):
                 to = at(2 * y_pair + rem(y_par + y_k, 2), z, 2 * rem(xx + x_k, X) + 1)
                 if y_k or x_k:
-                    send(mine.at[0], buf_a.at[slot_a], as_sem, a_sem, to)
+                    send(src, dst, as_sem.at[i], a_sem.at[i], to)
                 else:
                     @pl.when(main)
                     def _():
-                        pltpu.make_async_copy(mine.at[0], buf_a.at[slot_a], a_sem).start()
+                        pltpu.make_async_copy(src, dst, a_sem.at[i]).start()
 
                     @pl.when(aside)
                     def _(to=to):
-                        send(mine.at[0], buf_a.at[slot_a], as_sem, a_sem, to)
-
-    def second():
+                        send(src, dst, as_sem.at[i], a_sem.at[i], to)
+
+    def second(i):
         @pl.when(main)
         def _():
-            done(buf_a, a_sem)
-            mine[1] = summed([buf_a[s] for s in range(2 * L)])
+            done(buf_a.at[i], a_sem.at[i])
+            mine[i, 1] = summed([buf_a[i, s] for s in range(2 * L)])
+            src, dst = mine.at[i, 1], buf_b.at[i, slot_b]
             for y_k in (2, 1, 3, 0):
                 for z_k in near_last:
-                    for core in (0, 1):
+                    for core in (0, 1) if i == 2 else (1,):
                         if y_k or z_k or core == 0:
                             to = at(2 * rem(y_pair + y_k, Y // 2) + y_par, rem(z + z_k, Z), 2 * xx + core)
-                            send(mine.at[1], buf_b.at[slot_b], bs_sem, b_sem, to)
-            pltpu.make_async_copy(mine.at[1], buf_b.at[slot_b], b_sem).start()
-
-    def third():
-        done(buf_b, b_sem)
-        return summed([buf_b[s] for s in range(Z * Y // 2)])
-
-    def start(i, step, tile):
-        line[i, step] = tile
-        slot = (l, yy, z)[step]
-        for k in near_last[:-1]:
-            to = (at(yy, z, rem(l + k, L)), at(rem(yy + k, Y), z, l), at(yy, rem(z + k, Z), l))[step]
-            send(line.at[i, step], buf_c.at[i, step, slot], cs_sem.at[i, step], c_sem.at[i, step], to)
-        pltpu.make_async_copy(line.at[i, step], buf_c.at[i, step, slot], c_sem.at[i, step]).start()
-
-    def finish(i, step):
-        done(buf_c.at[i, step], c_sem.at[i, step])
-        return summed([buf_c[i, step, s] for s in range(8)])
+                            send(src, dst, bs_sem.at[i], b_sem.at[i], to)
+            pltpu.make_async_copy(src, dst, b_sem.at[i]).start()
+
+    def third(i):
+        if i == 2:
+            done(buf_b.at[i], b_sem.at[i])
+            return summed([buf_b[i, s] for s in range(Z * Y // 2)])
+
+        @pl.when(main)
+        def _():
+            done(buf_b.at[i], b_sem.at[i])
+            whole[i] = summed([buf_b[i, s] for s in range(Z * Y // 2)])
+            send(whole.at[i], whole.at[i], ws_sem.at[i], w_sem.at[i], at(yy, z, 2 * xx))
+
+        @pl.when(aside)
+        def _():
+            done(whole.at[i], w_sem.at[i])
+
+        return whole[i]
 
     @pl.when(reads)
     def _():
@@ -297,15 +300,14 @@
             def _(src=src, to=to):
                 send(src, got.at[l], ds_sem, d_sem, to)
 
-    start(0, 0, folded(nt(m_x, padded(xc)) + nt(xc, padded(m_x))))
-    start(0, 1, finish(0, 0))
+    first(0, folded(nt(m_x, padded(xc)) + nt(xc, padded(m_x))))
     @pl.when(main)
     def _():
         done(got, d_sem)
         part[...] = summed([got[s] for s in range(L)])
         send(part, other, os_sem, o_sem, (r, rem(y_hi + 1, YH) * L + l))
 
-    start(0, 2, finish(0, 1))
+    second(0)
 
     @pl.when(main)
     def _():
@@ -318,7 +320,7 @@
             send(piece, y.at[:, mine_of], ys_sem, y_sem, at(yy, z, rem(l + k, L)))
         pltpu.make_async_copy(piece, y.at[:, mine_of], y_sem).start()
 
-    theta = unfolded(finish(0, 2))[:, :K] / ROWS
+    theta = unfolded(third(0))[:, :K] / ROWS
     own = pl.ds(pl.multiple_of(c * SHARE, SHARE), SHARE)
 
     @pl.when(main)
@@ -334,7 +336,7 @@
     def _():
         products[...] = jnp.zeros_like(products)
 
-    start(1, 0, products[...])
+    first(1, products[...])
     taken = nn(theta, jnp.concatenate([m_x, xc, x[:, own]], 1))
 
     @pl.when(reads)
@@ -346,14 +348,13 @@
     y_row = blocks(y, row_at)
     m_r = jnp.concatenate([nn(y_row[n], h[n]) for n in range(NB)], 1) - taken[:, : NB * B]
 
+    second(1)
     done(y_far, yfar_sem)
     r_col = jnp.concatenate(blocks(y_far, col_at), 1) - taken[:, NB * B : 2 * NB * B]
     left, right = jnp.concatenate([m_r, m_x, m_p], 0), jnp.concatenate([r_col, xc, p_col], 0)
-    first(packed(nt(left, padded(right)) + nt(right, padded(left))))
-    start(1, 1, finish(1, 0))
-    second()
-    start(1, 2, finish(1, 1))
-    inverse = inverse_factor(symmetric(unpacked(finish(1, 2))) / ROWS)[:, :24]
+    first(2, packed(nt(left, padded(right)) + nt(right, padded(left))))
+    second(2)
+    inverse = inverse_factor(symmetric(unpacked(third(1))) / ROWS)[:, :24]
     q_ref[...] = nn(inverse, jnp.concatenate([y[:, own] - taken[:, 2 * NB * B :], x[:, own], p[:, own]], 0))
 
     @pl.when(reads)
@@ -367,31 +368,31 @@
             done(pick.at[i], fs_sem.at[i])
 
     done(got.at[pl.ds(0, X - 1)], ds_sem)
-    done(buf_a.at[pl.ds(0, L - 1)], as_sem)
+    for i in range(3):
+        done(buf_a.at[i, pl.ds(0, L - 1)], as_sem.at[i])
 
     @pl.when(aside)
     def _():
         done(got.at[0], ds_sem)
-        done(buf_a.at[0], as_sem)
+        for i in range(3):
+            done(buf_a.at[i, 0], as_sem.at[i])
 
     @pl.when(main)
     def _():
         done(part, os_sem)
         done(got, yfs_sem)
         done(got.at[pl.ds(0, L - 1)], ys_sem)
-
-    for step in range(3):
-        done(buf_c.at[0, step, pl.ds(0, 7)], cs_sem.at[0, step])
-    for step in range(3):
-        done(buf_c.at[1, step, pl.ds(0, 7)], cs_sem.at[1, step])
-
-    half_way = nn(inverse, unpacked(third())[:, :24] / ROWS)
+        for i in range(2):
+            done(buf_b.at[i, pl.ds(0, Z * Y // 2 - 1)], bs_sem.at[i])
+            done(whole.at[i], ws_sem.at[i])
+
+    half_way = nn(inverse, unpacked(third(2))[:, :24] / ROWS)
     ray_ref[...] = nt(half_way, inverse) + nt(inverse, half_way)
 
     @pl.when(main)
     def _():
-        done(buf_b, bs_sem)
-        done(buf_b.at[pl.ds(0, Z * Y // 2 - 1)], bs_sem)
+        done(buf_b.at[2], bs_sem.at[2])
+        done(buf_b.at[2, pl.ds(0, Z * Y // 2 - 1)], bs_sem.at[2])
 
 
 def body(hamiltonian_blocks, block_rows, block_cols, current_states, previous_steps):
@@ -422,13 +423,12 @@
             pltpu.VMEM((4, B), F32),
             pltpu.VMEM((K, SEG), F32),
             pltpu.VMEM((K, SEG), F32),
+            pltpu.VMEM((3, 2, 4, B), F32),
+            pltpu.VMEM((3, 2 * L, 4, B), F32),
+            pltpu.VMEM((3, Z * Y // 2, 4, B), F32),
             pltpu.VMEM((2, 4, B), F32),
-            pltpu.VMEM((2, 3, 4, B), F32),
-            pltpu.VMEM((2 * L, 4, B), F32),
-            pltpu.VMEM((Z * Y // 2, 4, B), F32),
-            pltpu.VMEM((2, 3, 8, 4, B), F32),
             dma((5,)), dma, dma, dma, dma, dma((2,)), dma((2,)), dma, dma, dma, dma,
-            dma, dma, dma, dma, dma, dma, dma((2, 3)), dma, dma, dma((2, 3)), regular, regular,
+            dma, dma, dma, dma, dma((3,)), dma((3,)), dma((2,)), dma((3,)), dma((3,)), dma((2,)), regular, regular,
         ],
         compiler_params=pltpu.CompilerParams(collective_id=0, has_side_effects=True, vmem_limit_bytes=62 * 1024 * 1024),
         name="lobpcg_step",

time: 60.2 us -> 58.3 us (0.968)
  Pallas kernels: 57.4 us -> 55.5 us
    pallas_call x1, Pallas kernels: 57.4 us -> 55.5 us  [body(): pl.pallas_call(kernel, out_shape=(jax.ShapeDtypeStruct((3 * K, SHARE), F3...]
where the time goes in v9:
time: 58.3 us; the launch traced here: 58.1 us
  Pallas kernels  55.5 us (95%)
  local copies, waits for them, and re-layouts  1.96 us (3%)
  between operations  0.65 us (1%)
    pallas_call x1, Pallas kernels, body(): pl.pallas_call(kernel, out_shape=(jax.ShapeDtypeStruct((3 * K, SHARE), F3...  55.5 us
    unnamed x4, local copies, waits for them, and re-layouts  1.96 us

profile of v9, /device:TPU:1, one launch (start us, length us, event | category | flops | bytes accessed | tf_op | source)
XLA Modules:
  0.0 58.1 jit_solution(1765790209147094335)
XLA Ops:
  0.6 55.5 %lobpcg_step.1 = (f32[24,256]{1,0:T(8,128)}, f32[24,24]{1,0:T(8,128)}) custom-call(s32[4]{0:T(128)} %bitcast.4, s32[4]{0:T(128)} %bitcast.5, f32[4,128,128]{2,1,0:T(8,128)} %bitcast.3, f32[8,4096]{1,0:T(8,128)} %x_ref.1, f32[8,4096]{1,0:T(8,128)} %p_ref.1), custom_call_target="tpu_custom_call" | custom-call | tf_op jit(solution)/shard_map/lobpcg_step/pallas_call | solution.py:401
  56.1 0.0 copy-start
  56.1 1.4 %copy.9 = f32[24,256]{1,0:T(8,128)} copy(f32[24,256]{1,0:T(8,128)} %get-tuple-element.4) | data formatting | bytes 49152
  57.5 0.0 copy-done
  57.5 0.6 %copy.10 = f32[24,24]{1,0:T(8,128)} copy(f32[24,24]{1,0:T(8,128)S(1)} %copy-done) | data formatting | bytes 4608
Async XLA Ops:
  56.1 1.4 %copy-start = (f32[24,24]{1,0:T(8,128)S(1)}, f32[24,24]{1,0:T(8,128)}, u32[]{:S(2)}) copy-start(f32[24,24]{1,0:T(8,128)} %get-tuple-element.5) | copy-start | bytes 6916

commit v10 on v9

--- a/solution.py
+++ b/solution.py
@@ -430,7 +430,7 @@
             dma((5,)), dma, dma, dma, dma, dma((2,)), dma((2,)), dma, dma, dma, dma,
             dma, dma, dma, dma, dma((3,)), dma((3,)), dma((2,)), dma((3,)), dma((3,)), dma((2,)), regular, regular,
         ],
-        compiler_params=pltpu.CompilerParams(collective_id=0, has_side_effects=True, vmem_limit_bytes=62 * 1024 * 1024),
+        compiler_params=pltpu.CompilerParams(collective_id=0, has_side_effects=True, vmem_limit_bytes=56426496),
         name="lobpcg_step",
     )(block_rows.reshape(NB), block_cols.reshape(NB), hamiltonian_blocks.reshape(NB, B, B), current_states, previous_steps)
 

time: 58.3 us -> 57.5 us (0.986)
  Pallas kernels: 55.5 us -> 54.9 us
    pallas_call x1, Pallas kernels: 55.5 us -> 54.9 us  [body(): pl.pallas_call(kernel, out_shape=(jax.ShapeDtypeStruct((3 * K, SHARE), F3...]
    unnamed x4 -> x6, local copies, waits for them, and re-layouts: 1.96 us -> 1.87 us
where the time goes in v10:
time: 57.5 us; the launch traced here: 57.4 us
  Pallas kernels  54.9 us (95%)
  local copies, waits for them, and re-layouts  1.87 us (3%)
  between operations  0.66 us (1%)
    pallas_call x1, Pallas kernels, body(): pl.pallas_call(kernel, out_shape=(jax.ShapeDtypeStruct((3 * K, SHARE), F3...  54.9 us
    unnamed x6, local copies, waits for them, and re-layouts  1.87 us

profile of v10, /device:TPU:1, one launch (start us, length us, event | category | flops | bytes accessed | tf_op | source)
XLA Modules:
  0.0 57.4 jit_solution(5579762412770828242)
XLA Ops:
  0.6 0.0 copy-start
  0.6 0.0 copy-start.1
  0.7 0.6 %copy-done = s32[1,1,4]{2,1,0:T(1,128)S(1)} copy-done((s32[1,1,4]{2,1,0:T(1,128)S(1)}, s32[1,1,4]{2,1,0:T(1,128)}, u32[]{:S(2)}) %copy-start) | copy-done | bytes 40
  1.3 0.0 copy-done.1
  1.3 54.9 %lobpcg_step.1 = (f32[24,256]{1,0:T(8,128)S(1)}, f32[24,24]{1,0:T(8,128)S(1)}) custom-call(s32[4]{0:T(128)S(1)} %bitcast.3, s32[4]{0:T(128)S(1)} %bitcast.4, f32[4,128,128]{2,1,0:T(8,128)} %bitcast.5, f32[8,4096]{1,0:T(8,128)} %x_ref.1, f32[8,4096]{1,0:T(8,128)} %p_ref.1), custom_call_target="tpu_custom_call" | custom-call | tf_op jit(solution)/shard_map/lobpcg_step/pallas_call | solution.py:401
  56.2 0.6 %copy.9 = f32[24,256]{1,0:T(8,128)} copy(f32[24,256]{1,0:T(8,128)S(1)} %get-tuple-element.4) | data formatting | bytes 49152
  56.8 0.6 %copy.10 = f32[24,24]{1,0:T(8,128)} copy(f32[24,24]{1,0:T(8,128)S(1)} %get-tuple-element.5) | data formatting | bytes 4608
Async XLA Ops:
  0.6 0.7 %copy-start = (s32[1,1,4]{2,1,0:T(1,128)S(1)}, s32[1,1,4]{2,1,0:T(1,128)}, u32[]{:S(2)}) copy-start(s32[1,1,4]{2,1,0:T(1,128)} %param.6) | copy-start | bytes 52
  0.6 0.7 %copy-start.1 = (s32[1,1,4]{2,1,0:T(1,128)S(1)}, s32[1,1,4]{2,1,0:T(1,128)}, u32[]{:S(2)}) copy-start(s32[1,1,4]{2,1,0:T(1,128)} %param.7) | copy-start | bytes 52

commit v11 on v10

--- a/solution.py
+++ b/solution.py
@@ -270,6 +270,7 @@
 
     xc = far[0]
     direct = [nt(xc[:, n * B : (n + 1) * B], h[n]) for n in range(NB)]
+    cross = folded(nt(m_x, padded(xc)) + nt(xc, padded(m_x)))
 
     @pl.when(reads)
     def _():
@@ -300,7 +301,7 @@
             def _(src=src, to=to):
                 send(src, got.at[l], ds_sem, d_sem, to)
 
-    first(0, folded(nt(m_x, padded(xc)) + nt(xc, padded(m_x))))
+    first(0, cross)
     @pl.when(main)
     def _():
         done(got, d_sem)
@@ -348,11 +349,11 @@
     y_row = blocks(y, row_at)
     m_r = jnp.concatenate([nn(y_row[n], h[n]) for n in range(NB)], 1) - taken[:, : NB * B]
 
-    second(1)
     done(y_far, yfar_sem)
     r_col = jnp.concatenate(blocks(y_far, col_at), 1) - taken[:, NB * B : 2 * NB * B]
     left, right = jnp.concatenate([m_r, m_x, m_p], 0), jnp.concatenate([r_col, xc, p_col], 0)
     first(2, packed(nt(left, padded(right)) + nt(right, padded(left))))
+    second(1)
     second(2)
     inverse = inverse_factor(symmetric(unpacked(third(1))) / ROWS)[:, :24]
     q_ref[...] = nn(inverse, jnp.concatenate([y[:, own] - taken[:, 2 * NB * B :], x[:, own], p[:, own]], 0))

time: 57.5 us -> 57.4 us (level)
  no operation moved by 1% of the time
where the time goes in v11:
time: 57.4 us; the launch traced here: 57.3 us
  Pallas kernels  54.8 us (95%)
  local copies, waits for them, and re-layouts  1.87 us (3%)
  between operations  0.66 us (1%)
    pallas_call x1, Pallas kernels, body(): pl.pallas_call(kernel, out_shape=(jax.ShapeDtypeStruct((3 * K, SHARE), F3...  54.8 us
    unnamed x6, local copies, waits for them, and re-layouts  1.87 us

profile of v11, /device:TPU:1, one launch (start us, length us, event | category | flops | bytes accessed | tf_op | source)
XLA Modules:
  0.0 57.3 jit_solution(10727984544224414868)
XLA Ops:
  0.6 0.0 copy-start
  0.6 0.0 copy-start.1
  0.7 0.6 %copy-done = s32[1,1,4]{2,1,0:T(1,128)S(1)} copy-done((s32[1,1,4]{2,1,0:T(1,128)S(1)}, s32[1,1,4]{2,1,0:T(1,128)}, u32[]{:S(2)}) %copy-start) | copy-done | bytes 40
  1.3 0.0 copy-done.1
  1.3 54.8 %lobpcg_step.1 = (f32[24,256]{1,0:T(8,128)S(1)}, f32[24,24]{1,0:T(8,128)S(1)}) custom-call(s32[4]{0:T(128)S(1)} %bitcast.3, s32[4]{0:T(128)S(1)} %bitcast.4, f32[4,128,128]{2,1,0:T(8,128)} %bitcast.5, f32[8,4096]{1,0:T(8,128)} %x_ref.1, f32[8,4096]{1,0:T(8,128)} %p_ref.1), custom_call_target="tpu_custom_call" | custom-call | tf_op jit(solution)/shard_map/lobpcg_step/pallas_call | solution.py:402
  56.1 0.6 %copy.9 = f32[24,256]{1,0:T(8,128)} copy(f32[24,256]{1,0:T(8,128)S(1)} %get-tuple-element.4) | data formatting | bytes 49152
  56.7 0.6 %copy.10 = f32[24,24]{1,0:T(8,128)} copy(f32[24,24]{1,0:T(8,128)S(1)} %get-tuple-element.5) | data formatting | bytes 4608
Async XLA Ops:
  0.6 0.7 %copy-start = (s32[1,1,4]{2,1,0:T(1,128)S(1)}, s32[1,1,4]{2,1,0:T(1,128)}, u32[]{:S(2)}) copy-start(s32[1,1,4]{2,1,0:T(1,128)} %param.6) | copy-start | bytes 52
  0.6 0.7 %copy-start.1 = (s32[1,1,4]{2,1,0:T(1,128)S(1)}, s32[1,1,4]{2,1,0:T(1,128)}, u32[]{:S(2)}) copy-start(s32[1,1,4]{2,1,0:T(1,128)} %param.7) | copy-start | bytes 52

commit v12 on v11

--- a/solution.py
+++ b/solution.py
@@ -93,7 +93,7 @@
 
 
 def kernel(rows_ref, cols_ref, h_ref, x_ref, p_ref, q_ref, ray_ref,
-           rows, cols, h, x, p, pick, far, asked, wanted, m, m_near, d, got, part, other, piece, products, y, y_far, mine,
+           rows, cols, h, x, p, pick, far, asked, wanted, m, m_near, d, got, part, other, piece, y, y_far, mine,
            buf_a, buf_b, whole, load_sem, m_sem, ms_sem, want_sem, wants_sem, f_sem, fs_sem, d_sem, ds_sem, o_sem, os_sem,
            y_sem, ys_sem, yfar_sem, yfs_sem, a_sem, b_sem, w_sem, as_sem, bs_sem, ws_sem, step2, step3):
     r, c = lax.axis_index("row"), lax.axis_index("col")
@@ -218,7 +218,7 @@
 
     def first(i, tile):
         mine[i, 0] = tile
-        src, dst = mine.at[i, 0], buf_a.at[i, slot_a]
+        src, dst = mine.at[i, 0], buf_a.at[i, y_par * X + xx if i == 1 else slot_a]
         for y_k in (1, 0):
             for x_k in (2, 1, 3, 0):
                 to = at(2 * y_pair + rem(y_par + y_k, 2), z, 2 * rem(xx + x_k, X) + 1)
@@ -236,8 +236,9 @@
     def second(i):
         @pl.when(main)
         def _():
-            done(buf_a.at[i], a_sem.at[i])
-            mine[i, 1] = summed([buf_a[i, s] for s in range(2 * L)])
+            members = L if i == 1 else 2 * L
+            done(buf_a.at[i, pl.ds(0, members)], a_sem.at[i])
+            mine[i, 1] = summed([buf_a[i, s] for s in range(members)])
             src, dst = mine.at[i, 1], buf_b.at[i, slot_b]
             for y_k in (2, 1, 3, 0):
                 for z_k in near_last:
@@ -331,13 +332,8 @@
         half_of = pl.ds(pl.multiple_of(y_hi * width, width), width)
         residual = piece[:, half_of] - nn(theta, x[:, half])
         basis = jnp.concatenate([residual, x[:, half], p[:, half]], 0)
-        products[...] = packed(nt(basis, padded(basis)))
-
-    @pl.when(aside)
-    def _():
-        products[...] = jnp.zeros_like(products)
-
-    first(1, products[...])
+        first(1, packed(nt(basis, padded(basis))))
+
     taken = nn(theta, jnp.concatenate([m_x, xc, x[:, own]], 1))
 
     @pl.when(reads)
@@ -369,18 +365,19 @@
             done(pick.at[i], fs_sem.at[i])
 
     done(got.at[pl.ds(0, X - 1)], ds_sem)
-    for i in range(3):
+    for i in (0, 2):
         done(buf_a.at[i, pl.ds(0, L - 1)], as_sem.at[i])
 
     @pl.when(aside)
     def _():
         done(got.at[0], ds_sem)
-        for i in range(3):
+        for i in (0, 2):
             done(buf_a.at[i, 0], as_sem.at[i])
 
     @pl.when(main)
     def _():
         done(part, os_sem)
+        done(buf_a.at[1, pl.ds(0, L - 1)], as_sem.at[1])
         done(got, yfs_sem)
         done(got.at[pl.ds(0, L - 1)], ys_sem)
         for i in range(2):
@@ -421,7 +418,6 @@
             pltpu.VMEM((K, OWNED), F32),
             pltpu.VMEM((K, OWNED), F32),
             pltpu.VMEM((K, OWNED), F32),
-            pltpu.VMEM((4, B), F32),
             pltpu.VMEM((K, SEG), F32),
             pltpu.VMEM((K, SEG), F32),
             pltpu.VMEM((3, 2, 4, B), F32),

time: 57.4 us -> 57.4 us (level)
  no operation moved by 1% of the time
where the time goes in v12:
time: 57.4 us; the launch traced here: 57.3 us
  Pallas kernels  54.7 us (95%)
  local copies, waits for them, and re-layouts  1.87 us (3%)
  between operations  0.66 us (1%)
    pallas_call x1, Pallas kernels, body(): pl.pallas_call(kernel, out_shape=(jax.ShapeDtypeStruct((3 * K, SHARE), F3...  54.7 us
    unnamed x6, local copies, waits for them, and re-layouts  1.87 us

profile of v12, /device:TPU:1, one launch (start us, length us, event | category | flops | bytes accessed | tf_op | source)
XLA Modules:
  0.0 57.3 jit_solution(4899850331299513313)
XLA Ops:
  0.6 0.0 copy-start
  0.6 0.0 copy-start.1
  0.7 0.6 %copy-done = s32[1,1,4]{2,1,0:T(1,128)S(1)} copy-done((s32[1,1,4]{2,1,0:T(1,128)S(1)}, s32[1,1,4]{2,1,0:T(1,128)}, u32[]{:S(2)}) %copy-start) | copy-done | bytes 40
  1.3 0.0 copy-done.1
  1.3 54.7 %lobpcg_step.1 = (f32[24,256]{1,0:T(8,128)S(1)}, f32[24,24]{1,0:T(8,128)S(1)}) custom-call(s32[4]{0:T(128)S(1)} %bitcast.3, s32[4]{0:T(128)S(1)} %bitcast.4, f32[4,128,128]{2,1,0:T(8,128)} %bitcast.5, f32[8,4096]{1,0:T(8,128)} %x_ref.1, f32[8,4096]{1,0:T(8,128)} %p_ref.1), custom_call_target="tpu_custom_call" | custom-call | tf_op jit(solution)/shard_map/lobpcg_step/pallas_call | solution.py:399
  56.0 0.6 %copy.9 = f32[24,256]{1,0:T(8,128)} copy(f32[24,256]{1,0:T(8,128)S(1)} %get-tuple-element.4) | data formatting | bytes 49152
  56.7 0.6 %copy.10 = f32[24,24]{1,0:T(8,128)} copy(f32[24,24]{1,0:T(8,128)S(1)} %get-tuple-element.5) | data formatting | bytes 4608
Async XLA Ops:
  0.6 0.7 %copy-start = (s32[1,1,4]{2,1,0:T(1,128)S(1)}, s32[1,1,4]{2,1,0:T(1,128)}, u32[]{:S(2)}) copy-start(s32[1,1,4]{2,1,0:T(1,128)} %param.6) | copy-start | bytes 52
  0.6 0.7 %copy-start.1 = (s32[1,1,4]{2,1,0:T(1,128)S(1)}, s32[1,1,4]{2,1,0:T(1,128)}, u32[]{:S(2)}) copy-start(s32[1,1,4]{2,1,0:T(1,128)} %param.7) | copy-start | bytes 52
